TPU v7x, 768 devices: a whole 4x8x12 slice. The times are simulated.
768 devices in a mesh: rows: 32 (over x, y_hi, core), rep: 24 (over z, y_lo).
Axes of the slice: x: 4, y: 8 (y_hi: 4, y_lo: 2; y = y_hi * 2 + y_lo), z: 12, core: 2. Of those that a mesh axis runs over, the one named last changes fastest.
Arguments:
- features: bfloat16 [24576, 128], P('rows'), may hold values from -6 to 6
- self_weight: bfloat16 [128, 256], replicated, may hold values from -0.5 to 0.5
- neigh_weight: bfloat16 [128, 256], replicated, may hold values from -3 to 3
- bias: float32 [256], replicated, may hold values from -3 to 3
- degree: int32 [24576], P(('rows', 'rep')), may hold values from 16 to 96
- cotangent: bfloat16 [24576, 256], P(('rows', 'rep')), may hold values from -6 to 6
- owners: int32 [24, 4], P('rep'), may hold values from 0 to 31, as said below
- tile_rows: int32 [32, 24, 4, 16], P('rows', 'rep'), may hold values from 0 to 5
- tile_cols: int32 [32, 24, 4, 16], P('rows', 'rep'), may hold values from 0 to 5
- tile_count: int32 [32, 24, 4], P('rows', 'rep'), may hold values from 2 to 16, as said below
- masks: int32 [32, 24, 4, 16, 128, 128], P('rows', 'rep'), may hold values 0 or 1
Outputs:
- hidden: bfloat16 [24576, 256], P(('rows', 'rep'))
- grad_self: float32 [128, 256], replicated
- grad_neigh: float32 [128, 256], replicated
- grad_bias: float32 [256], replicated
Inputs may be any that keep to these rules, and one draw needn't show every extreme that they name: Within one index of rep the 4 owners are different row blocks. Slots at and beyond tile_count of a list are empty. Some row blocks hold 16 live tiles in every list of every copy, the others at most 8; at least one row block is of the first kind.
All inputs are finite; a program needn't handle non-finite values. No bound on the sum of `masks` on one device may be relied on, other than what follows from the above.
Results may differ from a plain program's by a relative error of at most 0.014.
Values may be sent and summed in bfloat16 or wider, within the bound.
A program may use at most 32 MiB of HBM per device.

v0:
```python
import jax
import jax.numpy as jnp
from jax import lax
from jax.sharding import PartitionSpec as P


def spread(value, axis, source):
    kept = jnp.where(lax.axis_index(axis) == source, value, 0).astype(value.dtype)
    return lax.psum(kept, axis)


def body(
    features,
    self_weight,
    neigh_weight,
    bias,
    degree,
    cotangent,
    owners,
    tile_rows,
    tile_cols,
    tile_count,
    masks,
):
    rows_dev, width_in = features.shape
    tile_size = masks.shape[-1]
    row_tiles = rows_dev // tile_size
    sections = owners.shape[1]
    slot_count = masks.shape[3]
    tile_grid = jnp.arange(row_tiles)
    slot_ids = jnp.arange(slot_count)
    summed = jnp.zeros((rows_dev, width_in), jnp.float32)
    for section_num in range(sections):
        owner_rows = spread(features, "rows", owners[0, section_num])
        pieces = owner_rows.reshape(row_tiles, tile_size, width_in)[tile_cols[0, 0, section_num]]
        pattern = masks[0, 0, section_num].astype(jnp.bfloat16)
        products = jnp.einsum("kpq,kqf->kpf", pattern, pieces, preferred_element_type=jnp.float32)
        live_slot = slot_ids < tile_count[0, 0, section_num]
        placing = (
            (tile_rows[0, 0, section_num][:, None] == tile_grid[None, :]) & live_slot[:, None]
        ).astype(jnp.float32)
        summed = summed + jnp.einsum("kr,kpf->rpf", placing, products).reshape(rows_dev, width_in)
    copies = lax.axis_size("rep")
    share_rows = rows_dev // copies
    copy_index = lax.axis_index("rep")
    own_sum = lax.psum_scatter(summed, "rep", scatter_dimension=0, tiled=True)
    own_features = lax.dynamic_slice_in_dim(features, copy_index * share_rows, share_rows, 0)
    neigh_mean = (own_sum / degree.astype(jnp.float32)[:, None]).astype(jnp.bfloat16)
    pre = jnp.dot(own_features, self_weight, preferred_element_type=jnp.float32)
    pre = pre + jnp.dot(neigh_mean, neigh_weight, preferred_element_type=jnp.float32) + bias
    negative = jnp.minimum(pre, 0.0)
    hidden = jnp.where(pre > 0, pre, jnp.expm1(negative)).astype(jnp.bfloat16)
    slope = jnp.where(pre > 0, 1.0, jnp.exp(negative))
    grad_pre = cotangent.astype(jnp.float32) * slope
    grad_low = grad_pre.astype(jnp.bfloat16)
    part_self = jnp.dot(own_features.T, grad_low, preferred_element_type=jnp.float32)
    part_neigh = jnp.dot(neigh_mean.T, grad_low, preferred_element_type=jnp.float32)
    part_bias = jnp.sum(grad_pre, axis=0)
    grad_self, grad_neigh, grad_bias = lax.psum((part_self, part_neigh, part_bias), ("rows", "rep"))
    norm_scale = (rows_dev * lax.axis_size("rows")) ** (-0.5)
    return (hidden, grad_self * norm_scale, grad_neigh * norm_scale, grad_bias * norm_scale)


def solution(mesh):
    return jax.shard_map(
        body,
        mesh=mesh,
        in_specs=(
            P("rows", None),
            P(),
            P(),
            P(),
            P(("rows", "rep")),
            P(("rows", "rep"), None),
            P("rep", None),
            P("rows", "rep", None, None),
            P("rows", "rep", None, None),
            P("rows", "rep", None),
            P("rows", "rep", None, None, None, None),
        ),
        out_specs=(P(("rows", "rep"), None), P(), P(), P()),
        check_vma=False,
    )
```

profile of v0, /device:TPU:1, one launch (start us, length us, event | category | flops | bytes accessed | tf_op | source)
XLA Modules:
  0.0 1023.0 jit_solution(15580391989952587715)
XLA Ops:
  7.2 1.4 fusion.48
  11.2 1.8 broadcast_select_fusion
  13.1 1.4 fusion.47
  16.5 2.7 convert.6
  20.0 296.6 %all-reduce.7.cloned.1.call-done = (bf16[6,128,128]{2,1,0:T(8,128)(2,1)}, bf16[6,128,128]{2,1,0:T(8,128)(2,1)}, bf16[6,128,128]{2,1,0:T(8,128)(2,1)}, bf16[6,128,128]{2,1,0:T(8,128)(2,1)}) async-done(((bf16[6,128,128]{2,1,0:T(8,128)(2,1)}, bf16[6,128,128]{2,1,0:T(8,128)(2,1)}, bf16[6,128,128]{2,1,0:T(8,128)(2,1)}, bf16[6,128,128]{2,1,0:T(8,128)(2,1)}), (bf16[6,128,128]{2,1,0:T(8,128)(2,1)}, ...) | async-done | bytes 786448 | tf_op jit(solution)/shard_map/psum | solution.py:9
  316.6 1.6 gather_fusion
  319.1 2.4 gather_fusion.1
  321.5 1.6 fusion.8
  323.1 1.2 copy.17
  324.3 1.4 gather_fusion.2
  325.7 1.6 fusion.7
  327.2 1.2 copy.18
  328.5 1.4 gather_fusion.3
  329.9 1.6 fusion.6
  333.2 0.8 copy.15
  334.1 0.8 fusion.16
  335.0 86.5 %reduce-scatter.2.cloned.1.call-done = f32[32,128]{1,0:T(8,128)} async-done(((f32[768,128]{1,0:T(8,128)}), f32[32,128]{1,0:T(8,128)}) %reduce-scatter.2.cloned.1.call-update) | async-done | bytes 16400 | tf_op jit(solution)/shard_map/reduce_scatter | solution.py:46
  421.5 1.5 fusion.12
  423.0 1.5 fusion.14
  424.5 124.3 %psum.55 = f32[256]{0:T(256)S(1)} all-reduce(f32[256]{0:T(256)S(1)} %get-tuple-element.14), channel_id=1, replica_groups=mesh['rows'=32,'rep'=24] {'rows','rep'}, use_global_device_ids=true, to_apply=%region_8.9 | all-reduce | flops 256 | bytes 2048 | tf_op jit(solution)/shard_map/psum | solution.py:59
  548.8 1.6 fusion.44
  551.0 462.2 %all-reduce.5.cloned.1.call-done = (f32[128,256]{1,0:T(8,128)}, f32[128,256]{1,0:T(8,128)}) async-done(((f32[128,256]{1,0:T(8,128)}, f32[128,256]{1,0:T(8,128)}), (f32[128,256]{1,0:T(8,128)}, f32[128,256]{1,0:T(8,128)})) %all-reduce.5.cloned.1.call-update) | async-done | bytes 262160 | tf_op jit(solution)/shard_map/psum | solution.py:59
  1013.3 1.6 broadcast_multiply_fusion
  1014.9 1.6 broadcast_multiply_fusion.1
  (45 shorter events, 6.0 us)
Async XLA Ops:
  7.2 414.3 %copy-start = (bf16[128,256]{1,0:T(8,128)(2,1)S(1)}, bf16[128,256]{1,0:T(8,128)(2,1)}, u32[]{:S(2)}) copy-start(bf16[128,256]{1,0:T(8,128)(2,1)} %param.13) | copy-start | bytes 196612
  7.2 309.4 %all-reduce.7.cloned.1.call-start = ((), (), s32[]{:S(2)}) async-start(), calls=%async_computation.3 | async-start | bytes 1572864 | tf_op jit(solution)/shard_map/psum | solution.py:9
  13.1 408.4 %reduce-scatter.2.cloned.1.call-start = ((), (), s32[]{:S(2)}) async-start(), calls=%async_computation.1 | async-start | bytes 409600 | tf_op jit(solution)/shard_map/reduce_scatter | solution.py:46
  16.5 3.4 copy-start.7
  16.5 3.4 copy-start.8
  319.1 5.1 copy-start.4
  324.3 4.2 copy-start.3
  331.4 1.1 copy-start.1
  331.4 1.3 copy-start.2
  332.7 1.4 copy-start.10
  332.7 1.4 copy-start.6
  332.7 88.7 %copy-start.5 = (bf16[32,256]{1,0:T(8,128)(2,1)S(1)}, bf16[32,256]{1,0:T(8,128)(2,1)}, u32[]{:S(2)}) copy-start(bf16[32,256]{1,0:T(8,128)(2,1)} %param.16) | copy-start | bytes 49156
  332.8 88.7 %copy-start.9 = (f32[256]{0:T(256)S(1)}, f32[256]{0:T(256)}, u32[]{:S(2)}) copy-start(f32[256]{0:T(256)} %param.14) | copy-start | bytes 3076
  334.0 679.2 %all-reduce.5.cloned.1.call-start = ((), (), s32[]{:S(2)}) async-start(), calls=%async_computation.2 | async-start | bytes 524288 | tf_op jit(solution)/shard_map/psum | solution.py:59
Sparse Core Ops, SparseCore 0:
  13.2 303.3 all-reduce.6
  334.2 87.2 reduce-scatter.1
  550.6 462.6 all-reduce.4
where the time goes:
time: 1020 us
  waiting for transfers between devices  845 us (83%)
  blocking collectives  124 us (12%)
  between operations  16.6 us (2%)
  local copies, waits for them, and re-layouts  14.1 us (1%)
  matrix products  11.6 us (1%)
  other arithmetic  10.8 us (1%)
    psum x1, waiting for transfers between devices, body(): lax.psum((part_self, part_neigh, part_bias), ('rows', 'rep'))  462 us
    psum x1, waiting for transfers between devices, spread(): return lax.psum(kept, axis)  297 us
    psum x1, blocking collectives, body(): lax.psum((part_self, part_neigh, part_bias), ('rows', 'rep'))  124 us
    reduce_scatter x1, waiting for transfers between devices, body(): own_sum = lax.psum_scatter(summed, 'rep', scatter_dimension=0, tiled=True)  86.5 us
  transfers between devices with their start and end apart: 3, of which 3 were waited for; matrix products, arithmetic and copies ran while one was open for 1% of the time, Pallas kernels for 0%

commit v1 on v0

v1 whole, which is shorter than its diff:
```python
import functools

import jax
import jax.numpy as jnp
from jax import lax
from jax.experimental import pallas as pl
from jax.experimental.pallas import tpu as pltpu
from jax.sharding import PartitionSpec as P

MESH = pl.DeviceIdType.MESH
NX, NYH, NC, NZ, NYL = 4, 4, 2, 12, 2
NY = NYH * NYL
TILE = 128
RT = 6
SECTIONS = 4
SLOTS = 16
ROWS = 768
CHIPS = NX * NYH
PIECE = ROWS // CHIPS
SHARE = ROWS // (NZ * NYL)
F_IN = 128
F = 256
NODES = 24576
GROUP = NX * NC
F32 = jnp.float32
BF16 = jnp.bfloat16


def kernel(
    feat, w_self, w_neigh, bias, degree, cot, owners, trow, tcol, tcnt, masks,
    hidden, g_self, g_neigh, g_bias,
    mask_raw, mask_low, got1, give_core, got_core, feats, tiles, prods, acc, y_out, y_in,
    z_out, z_in, pre_own, m1, r1, m2, r2, m3, r3, m4, r4, m5, r5,
    mask_sem, s_send, s1_recv, core_recv, yrecv, xrecv, relay_recv, half_send, half_recv,
    yl_send, yl_recv, z_send, z_recv, g_send, g_recv,
):
    row, rep = lax.axis_index("rows"), lax.axis_index("rep")
    core = lax.rem(row, NC)
    chip = lax.div(row, NC)
    yh = lax.rem(chip, NYH)
    x = lax.div(chip, NYH)
    yl = lax.rem(rep, NYL)
    z = lax.div(rep, NYL)
    y = yh * NYL + yl
    other = 1 - core

    def dev(x_, yh_, c_, z_, yl_):
        return ((x_ * NYH + yh_) * NC + c_, z_ * NYL + yl_)

    def at_y(y_):
        return dev(x, lax.div(y_, NYL), core, z, lax.rem(y_, NYL))

    def at_group(k):
        return dev(lax.div(k, NC), yh, lax.rem(k, NC), z, yl)

    def send(src, dst, ssem, rsem, device):
        copy = pltpu.make_async_remote_copy(
            src_ref=src, dst_ref=dst, send_sem=ssem, recv_sem=rsem, device_id=device, device_id_type=MESH
        )
        copy.start()

    def arrived(buf, sem):
        pltpu.make_async_copy(buf, buf, sem).wait()

    core_mate = dev(x, yh, other, z, yl)
    yl_mate = dev(x, yh, core, z, 1 - yl)
    row_mates = [
        (lax.rem(x + dx, NX), lax.rem(yh + dy, NYH)) for dx in range(NX) for dy in range(NYH) if dx or dy
    ]
    me_k = x * NC + core

    barrier = pltpu.get_barrier_semaphore()

    def greet(device):
        pl.semaphore_signal(barrier, inc=1, device_id=device, device_id_type=MESH)

    for x_, yh_ in row_mates:
        greet(dev(x_, yh_, core, z, yl))
    for dx in range(NX):
        greet(dev(lax.rem(x + dx, NX), yh, other, z, yl))
    for dy in range(NYH):
        greet(dev(x, lax.rem(yh + dy, NYH), core, z, 1 - yl))
    for dz in range(1, NZ):
        greet(dev(x, yh, core, lax.rem(z + dz, NZ), yl))

    mask_copies = [
        pltpu.make_async_copy(masks.at[s], mask_raw.at[s], mask_sem.at[s]) for s in range(SECTIONS)
    ]
    for copy in mask_copies:
        copy.start()
    got1[chip] = feat[pl.ds(pl.multiple_of(chip * PIECE, 16), PIECE), :]
    pl.semaphore_wait(barrier, len(row_mates) + NX + NYH + NZ - 1)

    for x_, yh_ in row_mates:
        there = x_ * NYH + yh_
        send(
            feat.at[pl.ds(pl.multiple_of(there * PIECE, 16), PIECE), :],
            got1.at[chip], s_send.at[0], s1_recv, dev(x_, yh_, core, z, yl),
        )

    own = feat[pl.ds(pl.multiple_of(rep * SHARE, 16), SHARE), :]
    pre_own[...] = jnp.dot(own, w_self[...], preferred_element_type=F32) + bias[...]
    for s in range(SECTIONS):
        mask_copies[s].wait()

        def lower(k, carry, s=s):
            mask_low[s, k] = mask_raw[s, k].astype(F32).astype(BF16)
            return carry

        lax.fori_loop(0, SLOTS, lower, 0, unroll=2)

    arrived(got1.at[pl.ds(0, CHIPS - 1)], s1_recv)

    def chosen(s):
        owner = owners[0, s]
        piece = jnp.zeros((PIECE, F_IN), F32)
        for b in range(CHIPS):
            gap = owner - (NC * b + core)
            piece = piece + got1[b].astype(F32) * (1 - jnp.minimum(gap * gap, 1)).astype(F32)
        return piece

    for t in range(2):
        give_core[t] = chosen(2 * other + t).astype(BF16)
    send(give_core, got_core, s_send.at[1], core_recv, core_mate)
    arrived(got_core, core_recv)
    place = pl.ds(pl.multiple_of(chip * PIECE, 16), PIECE)
    for t in range(2):
        feats[2 * core + t, place, :] = (chosen(2 * core + t) + got_core[t].astype(F32)).astype(BF16)

    def part(x_, yh_):
        start = pl.multiple_of((x_ * NYH + yh_) * PIECE, 16)
        return feats.at[pl.ds(2 * core, 2), pl.ds(start, PIECE), :]

    def line(x_):
        start = pl.multiple_of(x_ * (NYH * PIECE), 16)
        return feats.at[pl.ds(2 * core, 2), pl.ds(start, NYH * PIECE), :]

    def half_line(t, x_):
        start = pl.multiple_of(x_ * (NYH * PIECE), 16)
        return feats.at[2 * core + t, pl.ds(start, NYH * PIECE), :]

    def half(t, x_, yh_):
        start = pl.multiple_of((x_ * NYH + yh_) * PIECE, 16)
        return feats.at[2 * core + t, pl.ds(start, PIECE), :]

    right, left, far = lax.rem(x + 1, NX), lax.rem(x + 3, NX), lax.rem(x + 2, NX)
    to_right, to_left = dev(right, yh, core, z, yl), dev(left, yh, core, z, yl)
    for dy in (2, 1, 3):
        yh_ = lax.rem(yh + dy, NYH)
        send(part(x, yh), part(x, yh), s_send.at[2], yrecv.at[dy], dev(x, yh_, core, z, yl))
    for dy in (0, 1, 3, 2):
        yh_ = lax.rem(yh + NYH - dy, NYH)
        if dy:
            arrived(part(x, yh_), yrecv.at[dy])
        send(part(x, yh_), part(x, yh_), s_send.at[3], xrecv.at[0, dy], to_right)
        send(part(x, yh_), part(x, yh_), s_send.at[3], xrecv.at[1, dy], to_left)
    send(line(x), line(x), half_send, half_recv.at[0], core_mate)
    for dy in (0, 1, 3, 2):
        yh_ = lax.rem(yh + NYH - dy, NYH)
        arrived(part(left, yh_), xrecv.at[0, dy])
        send(half(0, left, yh_), half(0, left, yh_), s_send.at[4], relay_recv.at[0], to_right)
        arrived(part(right, yh_), xrecv.at[1, dy])
        send(half(1, right, yh_), half(1, right, yh_), s_send.at[4], relay_recv.at[1], to_left)
    send(line(left), line(left), half_send, half_recv.at[1], core_mate)
    send(line(right), line(right), half_send, half_recv.at[2], core_mate)
    arrived(half_line(0, far), relay_recv.at[0])
    arrived(half_line(1, far), relay_recv.at[1])
    send(line(far), line(far), half_send, half_recv.at[3], core_mate)

    def multiply(s, base):
        for c in range(RT):
            tiles[c] = feats[s, TILE * c:TILE * c + TILE, :]

        def one(k, carry):
            prods[base + k] = jnp.dot(
                mask_low[s, k], tiles[tcol[0, 0, s, k]], preferred_element_type=F32
            )
            return carry

        lax.fori_loop(0, SLOTS, one, 0, unroll=2)

    def gather_tile(total, r, s, base):
        for k in range(SLOTS):
            gap = trow[0, 0, s, k] - r
            live = (1 - jnp.minimum(gap * gap, 1)) * jnp.minimum(jnp.maximum(tcnt[0, 0, s] - k, 0), 1)
            total = total + live.astype(F32) * prods[base + k]
        return total

    for t in range(2):
        multiply(2 * core + t, t * SLOTS)

    def first_half(r, carry):
        total = jnp.zeros((TILE, F_IN), F32)
        for t in range(2):
            total = gather_tile(total, r, 2 * core + t, t * SLOTS)
        acc[pl.ds(4 * r, 4)] = total.reshape(4, SHARE, F_IN)
        return carry

    lax.fori_loop(0, RT, first_half, 0)

    far_half = feats.at[pl.ds(2 * other, 2)]
    for n in range(4):
        arrived(far_half.at[:, pl.ds(0, NYH * PIECE), :], half_recv.at[n])
    for t in range(2):
        multiply(2 * other + t, t * SLOTS)

    def second_half(step, carry):
        r = lax.rem(lax.div(z, 2) + 1 + step, RT)
        total = acc[pl.ds(4 * r, 4)].reshape(TILE, F_IN)
        for t in range(2):
            total = gather_tile(total, r, 2 * other + t, t * SLOTS)
        acc[pl.ds(4 * r, 4)] = total.reshape(4, SHARE, F_IN)
        for h in range(2):
            y_out[2 * r + h] = acc[4 * r + 2 * h + 1 - yl].astype(BF16)
        send(y_out.at[pl.ds(2 * r, 2)], y_in.at[pl.ds(2 * r, 2)], yl_send, yl_recv.at[r], yl_mate)
        return carry

    lax.fori_loop(0, RT, second_half, 0)

    def to_z(step, carry):
        r = lax.rem(lax.div(z, 2) + 1 + step, RT)
        arrived(y_in.at[pl.ds(2 * r, 2)], yl_recv.at[r])
        for h in range(2):
            z_ = 2 * r + h
            both = acc[4 * r + 2 * h + yl] + y_in[z_].astype(F32)
            acc[4 * r + 2 * h + yl] = both
            z_out[z_] = both.astype(BF16)

            @pl.when(z_ != z)
            def _():
                send(z_out.at[z_], z_in.at[z], z_send, z_recv, dev(x, yh, core, z_, yl))

        return carry

    lax.fori_loop(0, RT, to_z, 0)
    z_in[z] = jnp.zeros((SHARE, F_IN), BF16)
    lanes = lax.broadcasted_iota(jnp.int32, (SHARE, SHARE), 1)
    subs = lax.broadcasted_iota(jnp.int32, (SHARE, SHARE), 0)
    deg = jnp.sum(jnp.where(lanes == subs, degree[...].astype(F32), 0.0), axis=1, keepdims=True)
    total = acc[2 * z + yl]
    arrived(z_in.at[pl.ds(0, NZ - 1)], z_recv)
    for z_ in range(NZ):
        total = total + z_in[z_].astype(F32)

    mean = (total / deg).astype(BF16)
    pre = pre_own[...] + jnp.dot(mean, w_neigh[...], preferred_element_type=F32)
    fall = jnp.exp(jnp.minimum(pre, 0.0))
    up = pre > 0
    hidden[...] = jnp.where(up, pre, fall - 1.0).astype(BF16)
    grad_pre = cot[...].astype(F32) * jnp.where(up, 1.0, fall)
    grad_low = grad_pre.astype(BF16)
    part_bias = jnp.sum(grad_pre, axis=0, keepdims=True)
    both = jnp.concatenate([own, mean], axis=1)
    part = lax.dot_general(both, grad_low, (((0,), (0,)), ((), ())), preferred_element_type=F32)
    line_ids = lax.broadcasted_iota(jnp.int32, (16, TILE), 0)
    bias_tile = jnp.where(
        line_ids == 0, part_bias[:, :TILE], jnp.where(line_ids == 1, part_bias[:, TILE:], 0.0)
    ).astype(BF16)
    for k in range(GROUP):
        m1[k, 0:32, :] = part[32 * k:32 * k + 32, :TILE].astype(BF16)
        m1[k, 32:64, :] = part[32 * k:32 * k + 32, TILE:].astype(BF16)
        m1[k, 64:80, :] = bias_tile
    for d in range(1, GROUP):
        k = lax.rem(me_k + d, GROUP)
        send(m1.at[k], r1.at[me_k], g_send.at[0], g_recv.at[0], at_group(k))
    r1[me_k] = m1[me_k]
    arrived(r1.at[pl.ds(0, GROUP - 1)], g_recv.at[0])
    level = r1[0].astype(F32)
    for k in range(1, GROUP):
        level = level + r1[k].astype(F32)
    for k in range(NY):
        m2[k] = jnp.concatenate([level[8 * k:8 * k + 8], level[64:72]], axis=0).astype(BF16)
    for d in range(1, NY):
        y_ = lax.rem(y + d, NY)
        send(m2.at[y_], r2.at[y], g_send.at[1], g_recv.at[1], at_y(y_))
    r2[y] = m2[y]
    arrived(r2.at[pl.ds(0, NY - 1)], g_recv.at[1])
    level = r2[0].astype(F32)
    for k in range(1, NY):
        level = level + r2[k].astype(F32)
    m3[...] = level.astype(BF16)
    for d in range(1, NZ):
        z_ = lax.rem(z + d, NZ)
        send(m3, r3.at[z], g_send.at[2], g_recv.at[2], dev(x, yh, core, z_, yl))
    r3[z] = m3[...]
    arrived(r3.at[pl.ds(0, NZ - 1)], g_recv.at[2])
    level = r3[0].astype(F32)
    for k in range(1, NZ):
        level = level + r3[k].astype(F32)
    norm = float(NODES) ** -0.5
    level = level * norm
    m4[...] = level[0:8]
    for d in range(1, NY):
        y_ = lax.rem(y + d, NY)
        send(m4, r4.at[y], g_send.at[3], g_recv.at[3], at_y(y_))
    r4[y] = level[0:8]
    g_bias[:, 0:TILE] = level[8:9]
    g_bias[:, TILE:F] = level[9:10]
    arrived(r4.at[pl.ds(0, NY - 1)], g_recv.at[3])
    m5[...] = r4[...].reshape(64, TILE).astype(BF16)
    for d in range(1, GROUP):
        k = lax.rem(me_k + d, GROUP)
        send(m5, r5.at[me_k], g_send.at[4], g_recv.at[4], at_group(k))
    r5[me_k] = m5[...]

    arrived(got1.at[pl.ds(0, CHIPS - 1)], s_send.at[0])
    arrived(give_core, s_send.at[1])
    arrived(feats.at[0, pl.ds(0, 6 * PIECE), :], s_send.at[2])
    arrived(feats.at[0], s_send.at[3])
    arrived(feats.at[0, pl.ds(0, 8 * PIECE), :], s_send.at[4])
    arrived(feats.at[pl.ds(0, 2)], half_send)
    arrived(y_out, yl_send)
    arrived(z_out.at[pl.ds(0, NZ - 1)], z_send)
    arrived(m1.at[pl.ds(0, GROUP - 1)], g_send.at[0])
    arrived(m2.at[pl.ds(0, NY - 1)], g_send.at[1])
    arrived(r3.at[pl.ds(0, NZ - 1)], g_send.at[2])
    arrived(r4.at[pl.ds(0, NY - 1)], g_send.at[3])
    arrived(r5.at[pl.ds(0, GROUP - 1)], g_send.at[4])

    arrived(r5.at[pl.ds(0, GROUP - 1)], g_recv.at[4])
    for k in range(GROUP):
        target = g_self if k < GROUP // 2 else g_neigh
        first = 32 * (k % (GROUP // 2))
        target[first:first + 32, 0:TILE] = r5[k, 0:32, :].astype(F32)
        target[first:first + 32, TILE:F] = r5[k, 32:64, :].astype(F32)


def body(
    features, self_weight, neigh_weight, bias, degree, cotangent, owners, tile_rows, tile_cols, tile_count, masks
):
    vmem = pl.BlockSpec(memory_space=pltpu.VMEM)
    smem = pl.BlockSpec(memory_space=pltpu.SMEM)
    dma = pltpu.SemaphoreType.DMA
    hidden, g_self, g_neigh, g_bias = pl.pallas_call(
        kernel,
        out_shape=(
            jax.ShapeDtypeStruct((SHARE, F), BF16),
            jax.ShapeDtypeStruct((F_IN, F), F32),
            jax.ShapeDtypeStruct((F_IN, F), F32),
            jax.ShapeDtypeStruct((1, F), F32),
        ),
        in_specs=[vmem] * 6 + [smem] * 4 + [pl.BlockSpec(memory_space=pl.ANY)],
        out_specs=(vmem,) * 4,
        scratch_shapes=[
            pltpu.VMEM((SECTIONS, SLOTS, TILE, TILE), jnp.int32),
            pltpu.VMEM((SECTIONS, SLOTS, TILE, TILE), BF16),
            pltpu.VMEM((CHIPS, PIECE, F_IN), BF16),
            pltpu.VMEM((2, PIECE, F_IN), BF16),
            pltpu.VMEM((2, PIECE, F_IN), BF16),
            pltpu.VMEM((SECTIONS, ROWS, F_IN), BF16),
            pltpu.VMEM((RT, TILE, F_IN), BF16),
            pltpu.VMEM((2 * SLOTS, TILE, F_IN), F32),
            pltpu.VMEM((NZ * NYL, SHARE, F_IN), F32),
            pltpu.VMEM((NZ, SHARE, F_IN), BF16),
            pltpu.VMEM((NZ, SHARE, F_IN), BF16),
            pltpu.VMEM((NZ, SHARE, F_IN), BF16),
            pltpu.VMEM((NZ, SHARE, F_IN), BF16),
            pltpu.VMEM((SHARE, F), F32),
            pltpu.VMEM((GROUP, 80, TILE), BF16),
            pltpu.VMEM((GROUP, 80, TILE), BF16),
            pltpu.VMEM((NY, 16, TILE), BF16),
            pltpu.VMEM((NY, 16, TILE), BF16),
            pltpu.VMEM((16, TILE), BF16),
            pltpu.VMEM((NZ, 16, TILE), BF16),
            pltpu.VMEM((8, TILE), F32),
            pltpu.VMEM((NY, 8, TILE), F32),
            pltpu.VMEM((64, TILE), BF16),
            pltpu.VMEM((GROUP, 64, TILE), BF16),
            dma((SECTIONS,)),
            dma((5,)),
            dma,
            dma,
            dma((NYH,)),
            dma((2, NYH)),
            dma((2,)),
            dma,
            dma((4,)),
            dma,
            dma((RT,)),
            dma,
            dma,
            dma((5,)),
            dma((5,)),
        ],
        compiler_params=pltpu.CompilerParams(
            collective_id=0, has_side_effects=True, vmem_limit_bytes=40 * 1024 * 1024
        ),
    )(
        features, self_weight, neigh_weight, bias.reshape(1, F), degree.reshape(1, SHARE), cotangent,
        owners, tile_rows, tile_cols, tile_count, masks.reshape(SECTIONS, SLOTS, TILE, TILE),
    )
    return hidden, g_self, g_neigh, g_bias.reshape(F)


def solution(mesh):
    return jax.shard_map(
        body,
        mesh=mesh,
        in_specs=(
            P("rows", None),
            P(),
            P(),
            P(),
            P(("rows", "rep")),
            P(("rows", "rep"), None),
            P("rep", None),
            P("rows", "rep", None, None),
            P("rows", "rep", None, None),
            P("rows", "rep", None),
            P("rows", "rep", None, None, None, None),
        ),
        out_specs=(P(("rows", "rep"), None), P(), P(), P()),
        check_vma=False,
    )
```

time: 1020 us -> 93.8 us (0.09)
  waiting for transfers between devices: 845 us -> 0 us
  blocking collectives: 124 us -> 0 us
  Pallas kernels: 0 us -> 80.7 us
  between operations: 16.6 us -> 0.66 us
  matrix products: 11.6 us -> 0 us
  other arithmetic: 10.8 us -> 0 us
    psum x2 -> x0, waiting for transfers between devices: 759 us -> none  [the longest x1 462 us: body(): lax.psum((part_self, part_neigh, part_bias), ('rows', 'rep'))]
    psum x1 -> x0, blocking collectives: 124 us -> none  [body(): lax.psum((part_self, part_neigh, part_bias), ('rows', 'rep'))]
    reduce_scatter x1 -> x0, waiting for transfers between devices: 86.5 us -> none  [body(): own_sum = lax.psum_scatter(summed, 'rep', scatter_dimension=0, tiled=True)]
    pallas_call x0 -> x1, Pallas kernels: none -> 80.7 us  [body(): pl.pallas_call(kernel, out_shape=(jax.ShapeDtypeStruct((SHARE, F), BF16),...]
    dot_general x12 -> x0, matrix products: 11.6 us -> none  [the longest x4 5.17 us: body(): jnp.einsum('kpq,kqf->kpf', pattern, pieces, preferred_element_type=jnp.fl...]
    unnamed x22 -> x26, local copies, waits for them, and re-layouts: 0.45 us -> 12 us
  transfers between devices with their start and end apart: 3 -> 0, of which waited for: 3 -> 0; matrix products, arithmetic and copies ran while one was open for 1% -> 0% of each run, Pallas kernels for 0% -> 0%
where the time goes in v1:
time: 93.8 us; the launch traced here: 93.4 us
  Pallas kernels  80.7 us (86%)
  local copies, waits for them, and re-layouts  12 us (13%)
    pallas_call x1, Pallas kernels, body(): pl.pallas_call(kernel, out_shape=(jax.ShapeDtypeStruct((SHARE, F), BF16),...  80.7 us
    unnamed x26, local copies, waits for them, and re-layouts  12 us

profile of v1, /device:TPU:1, one launch (start us, length us, event | category | flops | bytes accessed | tf_op | source)
XLA Modules:
  0.0 93.4 jit_solution(1068852287470716325)
XLA Ops:
  0.6 0.0 copy-start
  0.6 2.2 %copy-done = s32[1,1,4,16,128,128]{5,4,3,2,1,0:T(8,128)S(1)} copy-done((s32[1,1,4,16,128,128]{5,4,3,2,1,0:T(8,128)S(1)}, s32[1,1,4,16,128,128]{5,4,3,2,1,0:T(8,128)}, u32[]{:S(2)}) %copy-start) | copy-done | bytes 4194328
  2.8 0.0 copy-start.1
  2.8 0.9 copy-done.1
  3.8 0.0 copy-start.2
  3.8 0.8 copy-done.2
  4.6 0.0 copy-start.3
  4.6 0.8 copy-done.3
  5.4 0.0 copy-start.4
  5.4 0.7 copy-done.4
  6.1 0.0 copy-start.5
  6.2 0.7 copy-done.5
  6.8 0.0 copy-start.6
  6.8 0.7 copy-done.6
  7.5 0.0 copy-start.7
  7.5 0.7 copy-done.7
  8.2 0.7 copy-done.8
  8.9 0.7 copy-done.9
  9.5 0.7 copy-done.10
  10.2 80.7 %shard_map.138 = (bf16[32,256]{1,0:T(8,128)(2,1)S(1)}, f32[128,256]{1,0:T(8,128)S(1)}, f32[128,256]{1,0:T(8,128)S(1)}, f32[1,256]{1,0:T(1,128)S(1)}) custom-call(bf16[768,128]{1,0:T(8,128)(2,1)S(1)} %copy-done.1, bf16[128,256]{1,0:T(8,128)(2,1)S(1)} %copy-done.2, bf16[128,256]{1,0:T(8,128)(2,1)S(1)} %copy-done.3, f32[1,256]{1,0:T(1,128)S(1)} %bitcast.5, ...), custom_call_target="tpu_custom_call" | custom-call | tf_op jit(solution)/shard_map/pallas_call | solution.py:334
  90.9 0.6 copy.19
  91.5 0.7 copy.20
  92.1 0.7 copy.21
  92.8 0.6 copy.22
  (3 shorter events, 0.0 us)
Async XLA Ops:
  0.6 2.2 %copy-start = (s32[1,1,4,16,128,128]{5,4,3,2,1,0:T(8,128)S(1)}, s32[1,1,4,16,128,128]{5,4,3,2,1,0:T(8,128)}, u32[]{:S(2)}) copy-start(s32[1,1,4,16,128,128]{5,4,3,2,1,0:T(8,128)} %param.21) | copy-start | bytes 12582916
  2.8 0.9 copy-start.1
  3.8 0.8 copy-start.2
  4.6 0.8 copy-start.3
  5.4 0.7 copy-start.4
  6.1 0.7 copy-start.5
  6.8 0.7 copy-start.6
  7.5 0.7 copy-start.7
  8.2 0.7 copy-start.8
  8.8 0.7 copy-start.9
  9.5 0.7 copy-start.10

commit v2 on v1

--- a/solution.py
+++ b/solution.py
@@ -21,17 +21,18 @@
 F_IN = 128
 F = 256
 NODES = 24576
-GROUP = NX * NC
 F32 = jnp.float32
 BF16 = jnp.bfloat16
 
 
 def kernel(
-    feat, w_self, w_neigh, bias, degree, cot, owners, trow, tcol, tcnt, masks,
-    hidden, g_self, g_neigh, g_bias,
+    feat_h, w_self_h, w_neigh_h, bias_h, degree_h, cot_h, owners_h, trow_h, tcol_h, tcnt_h, masks,
+    hidden, grads, g_bias,
+    feat, w_self, w_neigh, bias, degree, cot, owners, trow, tcol, tcnt,
     mask_raw, mask_low, got1, give_core, got_core, feats, tiles, prods, acc, y_out, y_in,
-    z_out, z_in, pre_own, m1, r1, m2, r2, m3, r3, m4, r4, m5, r5,
-    mask_sem, s_send, s1_recv, core_recv, yrecv, xrecv, relay_recv, half_send, half_recv,
+    z_out, z_in, pre_own, pair_out, pair_in, bias_out, bias_in, bias_sum, bias_far,
+    m1, r1, m3, r3, m4, r4, r5,
+    in_sem, mask_sem, s_send, s1_recv, core_recv, yrecv, xrecv, far_recv, relay_recv, half_send, half_recv,
     yl_send, yl_recv, z_send, z_recv, g_send, g_recv,
 ):
     row, rep = lax.axis_index("rows"), lax.axis_index("rep")
@@ -47,11 +48,8 @@
     def dev(x_, yh_, c_, z_, yl_):
         return ((x_ * NYH + yh_) * NC + c_, z_ * NYL + yl_)
 
-    def at_y(y_):
-        return dev(x, lax.div(y_, NYL), core, z, lax.rem(y_, NYL))
-
-    def at_group(k):
-        return dev(lax.div(k, NC), yh, lax.rem(k, NC), z, yl)
+    def at_plane(x_, y_):
+        return dev(x_, lax.div(y_, NYL), core, z, lax.rem(y_, NYL))
 
     def send(src, dst, ssem, rsem, device):
         copy = pltpu.make_async_remote_copy(
@@ -64,40 +62,51 @@
 
     core_mate = dev(x, yh, other, z, yl)
     yl_mate = dev(x, yh, core, z, 1 - yl)
-    row_mates = [
-        (lax.rem(x + dx, NX), lax.rem(yh + dy, NYH)) for dx in range(NX) for dy in range(NYH) if dx or dy
-    ]
-    me_k = x * NC + core
-
+    plane = [(lax.rem(x + dx, NX), lax.rem(y + dy, NY)) for dx in (2, 1, 3, 0) for dy in (4, 3, 5, 2, 6, 1, 7, 0)]
+    plane = plane[:-1]
+    me_q = x * NY + y
+
+    pairs = (
+        (feat_h, feat), (owners_h, owners), (w_self_h, w_self), (bias_h, bias), (trow_h, trow), (tcol_h, tcol),
+        (tcnt_h, tcnt), (w_neigh_h, w_neigh), (degree_h, degree), (cot_h, cot),
+    )
+    loads = [pltpu.make_async_copy(a, b, in_sem.at[n]) for n, (a, b) in enumerate(pairs)]
+    for copy in loads:
+        copy.start()
     barrier = pltpu.get_barrier_semaphore()
 
     def greet(device):
         pl.semaphore_signal(barrier, inc=1, device_id=device, device_id_type=MESH)
 
-    for x_, yh_ in row_mates:
-        greet(dev(x_, yh_, core, z, yl))
-    for dx in range(NX):
-        greet(dev(lax.rem(x + dx, NX), yh, other, z, yl))
-    for dy in range(NYH):
-        greet(dev(x, lax.rem(yh + dy, NYH), core, z, 1 - yl))
-    for dz in range(1, NZ):
+    for dz in (6, 5, 7, 4, 8, 3, 9, 2, 10, 1, 11):
         greet(dev(x, yh, core, lax.rem(z + dz, NZ), yl))
+    for x_, y_ in plane:
+        greet(at_plane(x_, y_))
+    greet(core_mate)
 
     mask_copies = [
         pltpu.make_async_copy(masks.at[s], mask_raw.at[s], mask_sem.at[s]) for s in range(SECTIONS)
     ]
     for copy in mask_copies:
         copy.start()
+    loads[0].wait()
     got1[chip] = feat[pl.ds(pl.multiple_of(chip * PIECE, 16), PIECE), :]
-    pl.semaphore_wait(barrier, len(row_mates) + NX + NYH + NZ - 1)
-
-    for x_, yh_ in row_mates:
+    pl.semaphore_wait(barrier, len(plane) + NZ)
+
+    near, across = lax.rem(yh + 2 * yl + NYH - 1, NYH), lax.rem(yh + 2, NYH)
+    shares = [(2, across, 1 - yl), (1, across, 1 - yl), (3, across, 1 - yl), (0, across, 1 - yl)]
+    shares += [(dx, near, yl_) for dx in (2, 1, 3, 0) for yl_ in range(NYL)]
+    shares += [(dx, yh, yl) for dx in (2, 1, 3)]
+    for dx, yh_, yl_ in shares:
+        x_ = lax.rem(x + dx, NX)
         there = x_ * NYH + yh_
         send(
             feat.at[pl.ds(pl.multiple_of(there * PIECE, 16), PIECE), :],
-            got1.at[chip], s_send.at[0], s1_recv, dev(x_, yh_, core, z, yl),
+            got1.at[chip], s_send.at[0], s1_recv, dev(x_, yh_, core, z, yl_),
         )
 
+    for copy in loads[1:]:
+        copy.wait()
     own = feat[pl.ds(pl.multiple_of(rep * SHARE, 16), SHARE), :]
     pre_own[...] = jnp.dot(own, w_self[...], preferred_element_type=F32) + bias[...]
     for s in range(SECTIONS):
@@ -135,10 +144,6 @@
         start = pl.multiple_of(x_ * (NYH * PIECE), 16)
         return feats.at[pl.ds(2 * core, 2), pl.ds(start, NYH * PIECE), :]
 
-    def half_line(t, x_):
-        start = pl.multiple_of(x_ * (NYH * PIECE), 16)
-        return feats.at[2 * core + t, pl.ds(start, NYH * PIECE), :]
-
     def half(t, x_, yh_):
         start = pl.multiple_of((x_ * NYH + yh_) * PIECE, 16)
         return feats.at[2 * core + t, pl.ds(start, PIECE), :]
@@ -148,23 +153,30 @@
     for dy in (2, 1, 3):
         yh_ = lax.rem(yh + dy, NYH)
         send(part(x, yh), part(x, yh), s_send.at[2], yrecv.at[dy], dev(x, yh_, core, z, yl))
+    to_far = dev(far, yh, core, z, yl)
     for dy in (0, 1, 3, 2):
         yh_ = lax.rem(yh + NYH - dy, NYH)
         if dy:
             arrived(part(x, yh_), yrecv.at[dy])
+        if dy == 2:
+            send(part(x, yh_), part(x, yh_), s_send.at[3], far_recv, to_far)
         send(part(x, yh_), part(x, yh_), s_send.at[3], xrecv.at[0, dy], to_right)
         send(part(x, yh_), part(x, yh_), s_send.at[3], xrecv.at[1, dy], to_left)
     send(line(x), line(x), half_send, half_recv.at[0], core_mate)
     for dy in (0, 1, 3, 2):
         yh_ = lax.rem(yh + NYH - dy, NYH)
         arrived(part(left, yh_), xrecv.at[0, dy])
+        if dy == 2:
+            arrived(part(right, yh_), xrecv.at[1, dy])
+            break
         send(half(0, left, yh_), half(0, left, yh_), s_send.at[4], relay_recv.at[0], to_right)
         arrived(part(right, yh_), xrecv.at[1, dy])
         send(half(1, right, yh_), half(1, right, yh_), s_send.at[4], relay_recv.at[1], to_left)
     send(line(left), line(left), half_send, half_recv.at[1], core_mate)
     send(line(right), line(right), half_send, half_recv.at[2], core_mate)
-    arrived(half_line(0, far), relay_recv.at[0])
-    arrived(half_line(1, far), relay_recv.at[1])
+    arrived(feats.at[0, pl.ds(0, 3 * PIECE), :], relay_recv.at[0])
+    arrived(feats.at[0, pl.ds(0, 3 * PIECE), :], relay_recv.at[1])
+    arrived(part(far, across), far_recv)
     send(line(far), line(far), half_send, half_recv.at[3], core_mate)
 
     def multiply(s, base):
@@ -250,98 +262,104 @@
     grad_pre = cot[...].astype(F32) * jnp.where(up, 1.0, fall)
     grad_low = grad_pre.astype(BF16)
     part_bias = jnp.sum(grad_pre, axis=0, keepdims=True)
-    both = jnp.concatenate([own, mean], axis=1)
-    part = lax.dot_general(both, grad_low, (((0,), (0,)), ((), ())), preferred_element_type=F32)
-    line_ids = lax.broadcasted_iota(jnp.int32, (16, TILE), 0)
-    bias_tile = jnp.where(
-        line_ids == 0, part_bias[:, :TILE], jnp.where(line_ids == 1, part_bias[:, TILE:], 0.0)
-    ).astype(BF16)
-    for k in range(GROUP):
-        m1[k, 0:32, :] = part[32 * k:32 * k + 32, :TILE].astype(BF16)
-        m1[k, 32:64, :] = part[32 * k:32 * k + 32, TILE:].astype(BF16)
-        m1[k, 64:80, :] = bias_tile
-    for d in range(1, GROUP):
-        k = lax.rem(me_k + d, GROUP)
-        send(m1.at[k], r1.at[me_k], g_send.at[0], g_recv.at[0], at_group(k))
-    r1[me_k] = m1[me_k]
-    arrived(r1.at[pl.ds(0, GROUP - 1)], g_recv.at[0])
+    first_core = core == 0
+    pair_out[:, 0:F_IN] = jnp.where(first_core, mean, own)
+    pair_out[:, F_IN:] = grad_low
+    bias_out[...] = jnp.broadcast_to(
+        jnp.where(first_core, part_bias[:, F_IN:], part_bias[:, :F_IN]), (8, F_IN)
+    )
+    send(pair_out, pair_in, g_send.at[0], g_recv.at[0], core_mate)
+    send(bias_out, bias_in, g_send.at[1], g_recv.at[1], core_mate)
+    over_nodes = (((0,), (0,)), ((), ()))
+    part = lax.dot_general(jnp.where(first_core, own, mean), grad_low, over_nodes, preferred_element_type=F32)
+    half_bias = jnp.where(first_core, part_bias[:, :F_IN], part_bias[:, F_IN:])
+    arrived(pair_in, g_recv.at[0])
+    arrived(bias_in, g_recv.at[1])
+    part = part + lax.dot_general(
+        pair_in[:, 0:F_IN], pair_in[:, F_IN:], over_nodes, preferred_element_type=F32
+    )
+    line_ids = lax.broadcasted_iota(jnp.int32, (8, TILE), 0)
+    bias_tile = jnp.where(line_ids == 0, half_bias + bias_in[...], 0.0)
+    for q in range(NX * NY):
+        block = part[8 * (q // 2):8 * (q // 2) + 8, TILE * (q % 2):TILE * (q % 2) + TILE]
+        m1[q] = jnp.concatenate([block, bias_tile], axis=0).astype(BF16)
+    for x_, y_ in plane:
+        send(m1.at[x_ * NY + y_], r1.at[me_q], g_send.at[2], g_recv.at[2], at_plane(x_, y_))
+    r1[me_q] = m1[me_q]
+    arrived(r1.at[pl.ds(0, NX * NY - 1)], g_recv.at[2])
     level = r1[0].astype(F32)
-    for k in range(1, GROUP):
-        level = level + r1[k].astype(F32)
-    for k in range(NY):
-        m2[k] = jnp.concatenate([level[8 * k:8 * k + 8], level[64:72]], axis=0).astype(BF16)
-    for d in range(1, NY):
-        y_ = lax.rem(y + d, NY)
-        send(m2.at[y_], r2.at[y], g_send.at[1], g_recv.at[1], at_y(y_))
-    r2[y] = m2[y]
-    arrived(r2.at[pl.ds(0, NY - 1)], g_recv.at[1])
-    level = r2[0].astype(F32)
-    for k in range(1, NY):
-        level = level + r2[k].astype(F32)
+    for q in range(1, NX * NY):
+        level = level + r1[q].astype(F32)
     m3[...] = level.astype(BF16)
-    for d in range(1, NZ):
-        z_ = lax.rem(z + d, NZ)
-        send(m3, r3.at[z], g_send.at[2], g_recv.at[2], dev(x, yh, core, z_, yl))
+    for dz in (6, 5, 7, 4, 8, 3, 9, 2, 10, 1, 11):
+        send(m3, r3.at[z], g_send.at[3], g_recv.at[3], dev(x, yh, core, lax.rem(z + dz, NZ), yl))
     r3[z] = m3[...]
-    arrived(r3.at[pl.ds(0, NZ - 1)], g_recv.at[2])
+    arrived(r3.at[pl.ds(0, NZ - 1)], g_recv.at[3])
     level = r3[0].astype(F32)
     for k in range(1, NZ):
         level = level + r3[k].astype(F32)
-    norm = float(NODES) ** -0.5
-    level = level * norm
+    level = level * float(NODES) ** -0.5
     m4[...] = level[0:8]
-    for d in range(1, NY):
-        y_ = lax.rem(y + d, NY)
-        send(m4, r4.at[y], g_send.at[3], g_recv.at[3], at_y(y_))
-    r4[y] = level[0:8]
-    g_bias[:, 0:TILE] = level[8:9]
-    g_bias[:, TILE:F] = level[9:10]
-    arrived(r4.at[pl.ds(0, NY - 1)], g_recv.at[3])
-    m5[...] = r4[...].reshape(64, TILE).astype(BF16)
-    for d in range(1, GROUP):
-        k = lax.rem(me_k + d, GROUP)
-        send(m5, r5.at[me_k], g_send.at[4], g_recv.at[4], at_group(k))
-    r5[me_k] = m5[...]
+    for x_, y_ in plane:
+        send(m4, r4.at[me_q], g_send.at[4], g_recv.at[4], at_plane(x_, y_))
+    r4[me_q] = level[0:8]
+    bias_sum[...] = level[8:16]
+    send(bias_sum, bias_far, g_send.at[6], g_recv.at[6], core_mate)
+    arrived(r4.at[pl.ds(0, NX * NY - 1)], g_recv.at[4])
+    send(r4, r5, g_send.at[5], g_recv.at[5], core_mate)
+    for q in range(NX * NY):
+        grads[core, 8 * (q // 2):8 * (q // 2) + 8, TILE * (q % 2):TILE * (q % 2) + TILE] = r4[q]
 
     arrived(got1.at[pl.ds(0, CHIPS - 1)], s_send.at[0])
     arrived(give_core, s_send.at[1])
     arrived(feats.at[0, pl.ds(0, 6 * PIECE), :], s_send.at[2])
-    arrived(feats.at[0], s_send.at[3])
-    arrived(feats.at[0, pl.ds(0, 8 * PIECE), :], s_send.at[4])
+    arrived(feats.at[pl.ds(0, 3), pl.ds(0, 6 * PIECE), :], s_send.at[3])
+    arrived(feats.at[0, pl.ds(0, 6 * PIECE), :], s_send.at[4])
     arrived(feats.at[pl.ds(0, 2)], half_send)
     arrived(y_out, yl_send)
     arrived(z_out.at[pl.ds(0, NZ - 1)], z_send)
-    arrived(m1.at[pl.ds(0, GROUP - 1)], g_send.at[0])
-    arrived(m2.at[pl.ds(0, NY - 1)], g_send.at[1])
-    arrived(r3.at[pl.ds(0, NZ - 1)], g_send.at[2])
-    arrived(r4.at[pl.ds(0, NY - 1)], g_send.at[3])
-    arrived(r5.at[pl.ds(0, GROUP - 1)], g_send.at[4])
-
-    arrived(r5.at[pl.ds(0, GROUP - 1)], g_recv.at[4])
-    for k in range(GROUP):
-        target = g_self if k < GROUP // 2 else g_neigh
-        first = 32 * (k % (GROUP // 2))
-        target[first:first + 32, 0:TILE] = r5[k, 0:32, :].astype(F32)
-        target[first:first + 32, TILE:F] = r5[k, 32:64, :].astype(F32)
+    arrived(pair_out, g_send.at[0])
+    arrived(bias_out, g_send.at[1])
+    arrived(m1.at[pl.ds(0, NX * NY - 1)], g_send.at[2])
+    arrived(r3.at[pl.ds(0, NZ - 1)], g_send.at[3])
+    arrived(r4.at[pl.ds(0, NX * NY - 1)], g_send.at[4])
+    arrived(bias_sum, g_send.at[6])
+    arrived(r4, g_send.at[5])
+
+    arrived(bias_far, g_recv.at[6])
+    near_bias, far_bias = bias_sum[0:1, :], bias_far[0:1, :]
+    g_bias[:, 0:F_IN] = jnp.where(first_core, near_bias, far_bias)
+    g_bias[:, F_IN:] = jnp.where(first_core, far_bias, near_bias)
+    arrived(r5, g_recv.at[5])
+    for q in range(NX * NY):
+        grads[other, 8 * (q // 2):8 * (q // 2) + 8, TILE * (q % 2):TILE * (q % 2) + TILE] = r5[q]
 
 
 def body(
     features, self_weight, neigh_weight, bias, degree, cotangent, owners, tile_rows, tile_cols, tile_count, masks
 ):
     vmem = pl.BlockSpec(memory_space=pltpu.VMEM)
-    smem = pl.BlockSpec(memory_space=pltpu.SMEM)
     dma = pltpu.SemaphoreType.DMA
-    hidden, g_self, g_neigh, g_bias = pl.pallas_call(
+    hidden, grads, g_bias = pl.pallas_call(
         kernel,
         out_shape=(
             jax.ShapeDtypeStruct((SHARE, F), BF16),
-            jax.ShapeDtypeStruct((F_IN, F), F32),
-            jax.ShapeDtypeStruct((F_IN, F), F32),
+            jax.ShapeDtypeStruct((NC, F_IN, F), F32),
             jax.ShapeDtypeStruct((1, F), F32),
         ),
-        in_specs=[vmem] * 6 + [smem] * 4 + [pl.BlockSpec(memory_space=pl.ANY)],
-        out_specs=(vmem,) * 4,
+        in_specs=[pl.BlockSpec(memory_space=pl.ANY)] * 11,
+        out_specs=(vmem,) * 3,
         scratch_shapes=[
+            pltpu.VMEM((ROWS, F_IN), BF16),
+            pltpu.VMEM((F_IN, F), BF16),
+            pltpu.VMEM((F_IN, F), BF16),
+            pltpu.VMEM((1, F), F32),
+            pltpu.VMEM((1, SHARE), jnp.int32),
+            pltpu.VMEM((SHARE, F), BF16),
+            pltpu.SMEM((1, SECTIONS), jnp.int32),
+            pltpu.SMEM((1, 1, SECTIONS, SLOTS), jnp.int32),
+            pltpu.SMEM((1, 1, SECTIONS, SLOTS), jnp.int32),
+            pltpu.SMEM((1, 1, SECTIONS), jnp.int32),
             pltpu.VMEM((SECTIONS, SLOTS, TILE, TILE), jnp.int32),
             pltpu.VMEM((SECTIONS, SLOTS, TILE, TILE), BF16),
             pltpu.VMEM((CHIPS, PIECE, F_IN), BF16),
@@ -356,22 +374,27 @@
             pltpu.VMEM((NZ, SHARE, F_IN), BF16),
             pltpu.VMEM((NZ, SHARE, F_IN), BF16),
             pltpu.VMEM((SHARE, F), F32),
-            pltpu.VMEM((GROUP, 80, TILE), BF16),
-            pltpu.VMEM((GROUP, 80, TILE), BF16),
-            pltpu.VMEM((NY, 16, TILE), BF16),
-            pltpu.VMEM((NY, 16, TILE), BF16),
+            pltpu.VMEM((SHARE, F_IN + F), BF16),
+            pltpu.VMEM((SHARE, F_IN + F), BF16),
+            pltpu.VMEM((8, F_IN), F32),
+            pltpu.VMEM((8, F_IN), F32),
+            pltpu.VMEM((8, F_IN), F32),
+            pltpu.VMEM((8, F_IN), F32),
+            pltpu.VMEM((NX * NY, 16, TILE), BF16),
+            pltpu.VMEM((NX * NY, 16, TILE), BF16),
             pltpu.VMEM((16, TILE), BF16),
             pltpu.VMEM((NZ, 16, TILE), BF16),
             pltpu.VMEM((8, TILE), F32),
-            pltpu.VMEM((NY, 8, TILE), F32),
-            pltpu.VMEM((64, TILE), BF16),
-            pltpu.VMEM((GROUP, 64, TILE), BF16),
+            pltpu.VMEM((NX * NY, 8, TILE), F32),
+            pltpu.VMEM((NX * NY, 8, TILE), F32),
+            dma((10,)),
             dma((SECTIONS,)),
             dma((5,)),
             dma,
             dma,
             dma((NYH,)),
             dma((2, NYH)),
+            dma,
             dma((2,)),
             dma,
             dma((4,)),
@@ -379,17 +402,17 @@
             dma((RT,)),
             dma,
             dma,
-            dma((5,)),
-            dma((5,)),
+            dma((7,)),
+            dma((7,)),
         ],
         compiler_params=pltpu.CompilerParams(
-            collective_id=0, has_side_effects=True, vmem_limit_bytes=40 * 1024 * 1024
+            collective_id=0, has_side_effects=True, vmem_limit_bytes=60 * 1024 * 1024
         ),
     )(
         features, self_weight, neigh_weight, bias.reshape(1, F), degree.reshape(1, SHARE), cotangent,
         owners, tile_rows, tile_cols, tile_count, masks.reshape(SECTIONS, SLOTS, TILE, TILE),
     )
-    return hidden, g_self, g_neigh, g_bias.reshape(F)
+    return hidden, grads[0], grads[1], g_bias.reshape(F)
 
 
 def solution(mesh):

time: 93.8 us -> 82.9 us (0.88)
  local copies, waits for them, and re-layouts: 12 us -> 4.25 us
  Pallas kernels: 80.7 us -> 77.8 us
    unnamed x26 -> x2, local copies, waits for them, and re-layouts: 12 us -> 2.56 us
    pallas_call x1, Pallas kernels: 80.7 us -> 77.8 us  [body(): pl.pallas_call(kernel, out_shape=(jax.ShapeDtypeStruct((SHARE, F), BF16),...]
    squeeze x0 -> x1, local copies, waits for them, and re-layouts: none -> 1.69 us  [body(): return (hidden, grads[0], grads[1], g_bias.reshape(F))]
where the time goes in v2:
time: 82.9 us; the launch traced here: 82.6 us
  Pallas kernels  77.8 us (94%)
  local copies, waits for them, and re-layouts  4.25 us (5%)
    pallas_call x1, Pallas kernels, body(): pl.pallas_call(kernel, out_shape=(jax.ShapeDtypeStruct((SHARE, F), BF16),...  77.8 us
    unnamed x2, local copies, waits for them, and re-layouts  2.56 us
    squeeze x1, local copies, waits for them, and re-layouts, body(): return (hidden, grads[0], grads[1], g_bias.reshape(F))  1.69 us

profile of v2, /device:TPU:1, one launch (start us, length us, event | category | flops | bytes accessed | tf_op | source)
XLA Modules:
  0.0 82.6 jit_solution(3950218240613765028)
XLA Ops:
  0.6 77.8 %shard_map.138 = (bf16[32,256]{1,0:T(8,128)(2,1)}, f32[2,128,256]{2,1,0:T(8,128)}, f32[1,256]{1,0:T(1,128)}) custom-call(bf16[768,128]{1,0:T(8,128)(2,1)} %feat_h.1, bf16[128,256]{1,0:T(8,128)(2,1)} %w_self_h.1, bf16[128,256]{1,0:T(8,128)(2,1)} %w_neigh_h.1, f32[1,256]{1,0:T(1,128)} %bitcast.9, s32[1,32]{1,0:T(1,128)} %bitcast.11, bf16[32,256]{1,0:T(8,128)(2,1)} %cot_h.1, ...), custom_call_target="tpu_custom_call" | custom-call | tf_op jit(solution)/shard_map/pallas_call | solution.py:343
  78.4 1.7 %slice_bitcast_fusion = (f32[128,256]{1,0:T(8,128)}, f32[128,256]{1,0:T(8,128)}) fusion(f32[2,128,256]{2,1,0:T(8,128)} %get-tuple-element.8), kind=kLoop, calls=%fused_computation | loop fusion | bytes 524288 | tf_op jit(solution)/shard_map/squeeze | solution.py:415
  80.1 1.3 %copy.17 = bf16[32,256]{1,0:T(8,128)(2,1)} copy(bf16[32,256]{1,0:T(8,128)(2,1)} %get-tuple-element.16) | data formatting | bytes 32768
  81.4 1.2 %copy.18 = f32[256]{0:T(256)} copy(f32[256]{0:T(256)} %bitcast.10) | data formatting | bytes 2048

commit v3 on v2

v3 whole, which is shorter than its diff:
```python
import functools

import jax
import jax.numpy as jnp
from jax import lax
from jax.experimental import pallas as pl
from jax.experimental.pallas import tpu as pltpu
from jax.sharding import PartitionSpec as P

MESH = pl.DeviceIdType.MESH
NX, NYH, NC, NZ, NYL = 4, 4, 2, 12, 2
NY = NYH * NYL
TILE = 128
RT = 6
SECTIONS = 4
SLOTS = 16
ROWS = 768
CHIPS = NX * NYH
PIECE = ROWS // CHIPS
SHARE = ROWS // (NZ * NYL)
OWNERS = NX * NY // 2
F_IN = 128
F = 256
NODES = 24576
F32 = jnp.float32
BF16 = jnp.bfloat16


def kernel(
    feat_h, w_self_h, w_neigh_h, bias_h, degree_h, cot_h, owners_h, trow_h, tcol_h, tcnt_h, masks,
    hidden, grads, g_bias,
    feat, w_self, w_neigh, bias, degree, cot, owners, owners_v, owners_mate_v, owners_mate, trow, tcol, tcnt,
    before, last, mask_raw, mask_low, got1, give_core, got_core, feats, part_mate, tiles, sums, acc, y_out, y_in,
    z_out, z_in, pre_own, pair_out, pair_in, bias_out, bias_in, bias_sum, bias_far,
    m1, r1, m3, r3, m4, r4, r5, bias_tile, rb, m3b, r3b,
    in_sem, mask_sem, o_send, o_recv, o_copy, s_send, s1_recv, core_recv, yrecv, xrecv, far_recv, relay_recv, half_send, half_recv,
    yl_send, yl_recv, z_send, z_recv, g_send, g_recv,
):
    row, rep = lax.axis_index("rows"), lax.axis_index("rep")
    core = lax.rem(row, NC)
    chip = lax.div(row, NC)
    yh = lax.rem(chip, NYH)
    x = lax.div(chip, NYH)
    yl = lax.rem(rep, NYL)
    z = lax.div(rep, NYL)
    y = yh * NYL + yl
    other = 1 - core

    def dev(x_, yh_, c_, z_, yl_):
        return ((x_ * NYH + yh_) * NC + c_, z_ * NYL + yl_)

    def at_plane(x_, y_):
        return dev(x_, lax.div(y_, NYL), core, z, lax.rem(y_, NYL))

    def send(src, dst, ssem, rsem, device):
        copy = pltpu.make_async_remote_copy(
            src_ref=src, dst_ref=dst, send_sem=ssem, recv_sem=rsem, device_id=device, device_id_type=MESH
        )
        copy.start()

    def arrived(buf, sem):
        pltpu.make_async_copy(buf, buf, sem).wait()

    core_mate = dev(x, yh, other, z, yl)
    yl_mate = dev(x, yh, core, z, 1 - yl)
    plane = [(lax.rem(x + dx, NX), lax.rem(y + dy, NY)) for dx in (2, 1, 3, 0) for dy in (4, 3, 5, 2, 6, 1, 7, 0)]
    plane = plane[:-1]
    me_q = x * NY + y

    pairs = (
        (feat_h, feat), (owners_h, owners_v), (owners_h, owners), (w_self_h, w_self), (bias_h, bias), (trow_h, trow), (tcol_h, tcol),
        (tcnt_h, tcnt), (w_neigh_h, w_neigh), (degree_h, degree), (cot_h, cot),
    )
    loads = [pltpu.make_async_copy(a, b, in_sem.at[n]) for n, (a, b) in enumerate(pairs)]
    for copy in loads:
        copy.start()
    barrier = pltpu.get_barrier_semaphore()

    def greet(device):
        pl.semaphore_signal(barrier, inc=1, device_id=device, device_id_type=MESH)

    for dz in (6, 5, 7, 4, 8, 3, 9, 2, 10, 1, 11):
        greet(dev(x, yh, core, lax.rem(z + dz, NZ), yl))
    for x_, y_ in plane:
        greet(at_plane(x_, y_))
    greet(core_mate)

    mask_copies = [
        pltpu.make_async_copy(masks.at[s], mask_raw.at[s], mask_sem.at[s]) for s in range(SECTIONS)
    ]
    for copy in mask_copies:
        copy.start()
    loads[0].wait()
    loads[1].wait()
    loads[2].wait()
    got1[chip] = feat[pl.ds(pl.multiple_of(chip * PIECE, 16), PIECE), :]
    pl.semaphore_wait(barrier, len(plane) + NZ)

    send(owners_v, owners_mate_v, o_send, o_recv, yl_mate)
    near, across = lax.rem(yh + 2 * yl + NYH - 1, NYH), lax.rem(yh + 2, NYH)
    shares = [(2, across, 1 - yl), (1, across, 1 - yl), (3, across, 1 - yl), (0, across, 1 - yl)]
    shares += [(dx, near, yl_) for dx in (2, 1, 3, 0) for yl_ in range(NYL)]
    shares += [(dx, yh, yl) for dx in (2, 1, 3)]
    for dx, yh_, yl_ in shares:
        x_ = lax.rem(x + dx, NX)
        there = x_ * NYH + yh_
        send(
            feat.at[pl.ds(pl.multiple_of(there * PIECE, 16), PIECE), :],
            got1.at[chip], s_send.at[0], s1_recv, dev(x_, yh_, core, z, yl_),
        )

    for copy in loads[3:]:
        copy.wait()
    own = feat[pl.ds(pl.multiple_of(rep * SHARE, 16), SHARE), :]
    pre_own[...] = jnp.dot(own, w_self[...], preferred_element_type=F32) + bias[...]
    for s in range(SECTIONS):
        mask_copies[s].wait()

        def lower(k, carry, s=s):
            mask_low[s, k] = mask_raw[s, k].astype(F32).astype(BF16)
            return carry

        lax.fori_loop(0, SLOTS, lower, 0, unroll=2)

    def chain(t, ends):
        s = lax.rem(2 * core + t, SECTIONS)
        count = tcnt[0, 0, s]
        ends = list(ends)
        for k in range(SLOTS):
            live = jnp.minimum(jnp.maximum(count - k, 0), 1)
            spot = 1 + t * SLOTS + k
            link = 0
            for r in range(RT):
                gap = trow[0, 0, s, k] - r
                same = live * (1 - jnp.minimum(gap * gap, 1))
                link = link + same * ends[r]
                ends[r] = ends[r] + same * (spot - ends[r])
            before[t, k] = link
        return tuple(ends)

    ends = lax.fori_loop(0, SECTIONS, chain, (jnp.int32(0),) * RT)
    for r in range(RT):
        last[r] = ends[r]
    sums[0] = jnp.zeros((TILE, F_IN), F32)
    arrived(owners_mate_v, o_recv)
    fetch = pltpu.make_async_copy(owners_mate_v, owners_mate, o_copy)
    fetch.start()
    fetch.wait()
    arrived(got1.at[pl.ds(0, CHIPS - 1)], s1_recv)

    def chosen(table, s):
        owner = table[0, s]
        piece = jnp.zeros((PIECE, F_IN), F32)
        for b in range(CHIPS):
            gap = owner - (NC * b + core)
            piece = piece + got1[b].astype(F32) * (1 - jnp.minimum(gap * gap, 1)).astype(F32)
        return piece

    for t in range(2):
        give_core[0, t] = chosen(owners, 2 * other + t).astype(BF16)
        give_core[1, t] = chosen(owners_mate, 2 * other + t).astype(BF16)
    send(give_core, got_core, s_send.at[1], core_recv, core_mate)
    mine = [chosen(table, 2 * core + t) for table in (owners, owners_mate) for t in range(2)]
    arrived(got_core, core_recv)
    place = pl.ds(pl.multiple_of(chip * PIECE, 16), PIECE)
    for t in range(2):
        feats[2 * core + t, place, :] = (mine[t] + got_core[0, t].astype(F32)).astype(BF16)
        part_mate[t] = (mine[2 + t] + got_core[1, t].astype(F32)).astype(BF16)

    here = feats.at[pl.ds(2 * core, 2), place, :]

    def line(x_):
        start = pl.multiple_of(x_ * (NYH * PIECE), 16)
        return feats.at[pl.ds(2 * core, 2), pl.ds(start, NYH * PIECE), :]

    def part(x_, yh_):
        start = pl.multiple_of((x_ * NYH + yh_) * PIECE, 16)
        return feats.at[pl.ds(2 * core, 2), pl.ds(start, PIECE), :]

    def half(t, x_, yh_):
        start = pl.multiple_of((x_ * NYH + yh_) * PIECE, 16)
        return feats.at[2 * core + t, pl.ds(start, PIECE), :]

    right, left, far = lax.rem(x + 1, NX), lax.rem(x + 3, NX), lax.rem(x + 2, NX)
    to_right, to_left, to_far = (dev(x_, yh, core, z, yl) for x_ in (right, left, far))
    beside = lax.rem(yh + 1 - 2 * yl + NYH, NYH)
    send(part_mate, here, s_send.at[2], yrecv.at[2], dev(x, across, core, z, 1 - yl))
    send(part_mate, here, s_send.at[2], yrecv.at[0], dev(x, near, core, z, 1 - yl))
    send(here, here, s_send.at[2], yrecv.at[1], dev(x, near, core, z, yl))

    def sideways(n, yh_):
        send(part(x, yh_), part(x, yh_), s_send.at[3], xrecv.at[0, n], to_right)
        send(part(x, yh_), part(x, yh_), s_send.at[3], xrecv.at[1, n], to_left)

    def relay(n, yh_):
        arrived(part(left, yh_), xrecv.at[0, n])
        send(half(0, left, yh_), half(0, left, yh_), s_send.at[4], relay_recv.at[0], to_right)
        arrived(part(right, yh_), xrecv.at[1, n])
        send(half(1, right, yh_), half(1, right, yh_), s_send.at[4], relay_recv.at[1], to_left)

    sideways(0, yh)
    arrived(part(x, near), yrecv.at[0])
    sideways(1, near)
    relay(0, yh)
    arrived(part(x, beside), yrecv.at[1])
    sideways(2, beside)
    arrived(part(x, across), yrecv.at[2])
    send(part(x, across), part(x, across), s_send.at[3], far_recv, to_far)
    sideways(3, across)
    send(line(x), line(x), half_send, half_recv.at[0], core_mate)
    relay(1, near)
    relay(2, beside)
    arrived(part(left, across), xrecv.at[0, 3])
    send(line(left), line(left), half_send, half_recv.at[1], core_mate)
    arrived(part(right, across), xrecv.at[1, 3])
    send(line(right), line(right), half_send, half_recv.at[2], core_mate)
    arrived(part(far, across), far_recv)
    arrived(feats.at[0, pl.ds(0, 3 * PIECE), :], relay_recv.at[0])
    arrived(feats.at[0, pl.ds(0, 3 * PIECE), :], relay_recv.at[1])
    send(line(far), line(far), half_send, half_recv.at[3], core_mate)

    def multiply(t):
        s = lax.rem(2 * core + t, SECTIONS)
        for c in range(RT):
            tiles[c] = feats[s, TILE * c:TILE * c + TILE, :]

        def one(k, carry):
            product = jnp.dot(mask_low[s, k], tiles[tcol[0, 0, s, k]], preferred_element_type=F32)
            sums[1 + t * SLOTS + k] = product + sums[before[t, k]]
            return carry

        lax.fori_loop(0, SLOTS, one, 0, unroll=8)

    multiply(0)
    multiply(1)
    far_half = feats.at[pl.ds(2 * other, 2)]
    for n in range(4):
        arrived(far_half.at[:, pl.ds(0, NYH * PIECE), :], half_recv.at[n])
    multiply(2)
    multiply(3)

    def second_half(step, carry):
        r = lax.rem(lax.div(z, 2) + 1 + step, RT)
        acc[pl.ds(4 * r, 4)] = sums[last[r]].reshape(4, SHARE, F_IN)
        for h in range(2):
            y_out[2 * r + h] = acc[4 * r + 2 * h + 1 - yl].astype(BF16)
        send(y_out.at[pl.ds(2 * r, 2)], y_in.at[pl.ds(2 * r, 2)], yl_send, yl_recv.at[r], yl_mate)
        return carry

    lax.fori_loop(0, RT, second_half, 0)

    def to_z(step, carry):
        r = lax.rem(lax.div(z, 2) + 1 + step, RT)
        arrived(y_in.at[pl.ds(2 * r, 2)], yl_recv.at[r])
        for h in range(2):
            z_ = 2 * r + h
            both = acc[4 * r + 2 * h + yl] + y_in[z_].astype(F32)
            acc[4 * r + 2 * h + yl] = both
            z_out[z_] = both.astype(BF16)

            @pl.when(z_ != z)
            def _():
                send(z_out.at[z_], z_in.at[z], z_send, z_recv, dev(x, yh, core, z_, yl))

        return carry

    lax.fori_loop(0, RT, to_z, 0)
    z_in[z] = jnp.zeros((SHARE, F_IN), BF16)
    lanes = lax.broadcasted_iota(jnp.int32, (SHARE, SHARE), 1)
    subs = lax.broadcasted_iota(jnp.int32, (SHARE, SHARE), 0)
    deg = jnp.sum(jnp.where(lanes == subs, degree[...].astype(F32), 0.0), axis=1, keepdims=True)
    total = acc[2 * z + yl]
    arrived(z_in.at[pl.ds(0, NZ - 1)], z_recv)
    for z_ in range(NZ):
        total = total + z_in[z_].astype(F32)

    mean = (total / deg).astype(BF16)
    pre = pre_own[...] + jnp.dot(mean, w_neigh[...], preferred_element_type=F32)
    fall = jnp.exp(jnp.minimum(pre, 0.0))
    up = pre > 0
    hidden[...] = jnp.where(up, pre, fall - 1.0).astype(BF16)
    grad_pre = cot[...].astype(F32) * jnp.where(up, 1.0, fall)
    grad_low = grad_pre.astype(BF16)
    part_bias = jnp.sum(grad_pre, axis=0, keepdims=True)
    first_core = core == 0
    pair_out[:, 0:F_IN] = jnp.where(first_core, mean, own)
    pair_out[:, F_IN:] = grad_low
    bias_out[...] = jnp.broadcast_to(
        jnp.where(first_core, part_bias[:, F_IN:], part_bias[:, :F_IN]), (8, F_IN)
    )
    send(pair_out, pair_in, g_send.at[0], g_recv.at[0], core_mate)
    send(bias_out, bias_in, g_send.at[1], g_recv.at[1], core_mate)
    over_nodes = (((0,), (0,)), ((), ()))
    part = lax.dot_general(jnp.where(first_core, own, mean), grad_low, over_nodes, preferred_element_type=F32)
    half_bias = jnp.where(first_core, part_bias[:, :F_IN], part_bias[:, F_IN:])
    arrived(pair_in, g_recv.at[0])
    arrived(bias_in, g_recv.at[1])
    part = part + lax.dot_general(
        pair_in[:, 0:F_IN], pair_in[:, F_IN:], over_nodes, preferred_element_type=F32
    )
    bias_tile[...] = half_bias + bias_in[...]
    for o in range(OWNERS):
        m1[o] = part[16 * (o // 2):16 * (o // 2) + 16, TILE * (o % 2):TILE * (o % 2) + TILE].astype(BF16)
    pair_y = lax.div(y, 2)
    me_o = x * (NY // 2) + pair_y
    is_owner = lax.rem(y, 2) == core
    no_owner = lax.rem(y, 2) != core
    is_home = me_q == other
    no_home = me_q != other
    home = at_plane(0, other)
    for dx in (2, 1, 3, 0):
        for k in (2, 1, 3, 0):
            x_, h_ = lax.rem(x + dx, NX), lax.rem(pair_y + k, NY // 2)
            o_, device = x_ * (NY // 2) + h_, at_plane(x_, 2 * h_ + core)
            if dx or k:
                send(m1.at[o_], r1.at[me_q], g_send.at[2], g_recv.at[2], device)
            else:
                @pl.when(no_owner)
                def _():
                    send(m1.at[o_], r1.at[me_q], g_send.at[2], g_recv.at[2], device)

    @pl.when(no_home)
    def _():
        send(bias_tile, rb.at[me_q], g_send.at[7], g_recv.at[7], home)

    far_z = (6, 5, 7, 4, 8, 3, 9, 2, 10, 1, 11)
    norm = float(NODES) ** -0.5

    @pl.when(is_owner)
    def _():
        r1[me_q] = m1[me_o]
        arrived(r1.at[pl.ds(0, NX * NY - 1)], g_recv.at[2])
        level = r1[0].astype(F32)
        for q in range(1, NX * NY):
            level = level + r1[q].astype(F32)
        m3[...] = level.astype(BF16)
        for dz in far_z:
            send(m3, r3.at[z], g_send.at[3], g_recv.at[3], dev(x, yh, core, lax.rem(z + dz, NZ), yl))
        r3[z] = m3[...]
        arrived(r3.at[pl.ds(0, NZ - 1)], g_recv.at[3])
        level = r3[0].astype(F32)
        for k in range(1, NZ):
            level = level + r3[k].astype(F32)
        m4[...] = (level * norm).astype(BF16)
        for x_, y_ in plane:
            send(m4, r4.at[me_o], g_send.at[4], g_recv.at[4], at_plane(x_, y_))
        r4[me_o] = m4[...]
        arrived(r4.at[pl.ds(0, OWNERS - 1)], g_recv.at[4])

    @pl.when(is_home)
    def _():
        rb[me_q] = bias_tile[...]
        arrived(rb.at[pl.ds(0, NX * NY - 1)], g_recv.at[7])
        level = rb[0]
        for q in range(1, NX * NY):
            level = level + rb[q]
        m3b[...] = level
        for dz in far_z:
            send(m3b, r3b.at[z], g_send.at[8], g_recv.at[8], dev(x, yh, core, lax.rem(z + dz, NZ), yl))
        r3b[z] = level
        arrived(r3b.at[pl.ds(0, NZ - 1)], g_recv.at[8])
        level = r3b[0]
        for k in range(1, NZ):
            level = level + r3b[k]
        bias_sum[...] = level * norm
        for x_, y_ in plane:
            send(bias_sum, bias_sum, g_send.at[9], g_recv.at[9], at_plane(x_, y_))

    @pl.when(no_home)
    def _():
        arrived(bias_sum, g_recv.at[9])

    send(bias_sum, bias_far, g_send.at[6], g_recv.at[6], core_mate)

    @pl.when(no_owner)
    def _():
        arrived(r4, g_recv.at[4])

    send(r4, r5, g_send.at[5], g_recv.at[5], core_mate)
    grads[core] = r4[...]

    arrived(owners_v, o_send)
    arrived(got1.at[pl.ds(0, CHIPS - 1)], s_send.at[0])
    arrived(give_core, s_send.at[1])
    arrived(feats.at[0, pl.ds(0, 6 * PIECE), :], s_send.at[2])
    arrived(feats.at[pl.ds(0, 3), pl.ds(0, 6 * PIECE), :], s_send.at[3])
    arrived(feats.at[0, pl.ds(0, 6 * PIECE), :], s_send.at[4])
    arrived(feats.at[pl.ds(0, 2)], half_send)
    arrived(y_out, yl_send)
    arrived(z_out.at[pl.ds(0, NZ - 1)], z_send)
    arrived(pair_out, g_send.at[0])
    arrived(bias_out, g_send.at[1])
    @pl.when(is_owner)
    def _():
        arrived(m1.at[pl.ds(0, OWNERS - 1)], g_send.at[2])
        arrived(r3.at[pl.ds(0, NZ - 1)], g_send.at[3])
        arrived(r1.at[pl.ds(0, NX * NY - 1)], g_send.at[4])

    @pl.when(no_owner)
    def _():
        arrived(m1, g_send.at[2])

    @pl.when(is_home)
    def _():
        arrived(r3b.at[pl.ds(0, NZ - 1)], g_send.at[8])
        arrived(rb.at[pl.ds(0, NX * NY - 1)], g_send.at[9])

    @pl.when(no_home)
    def _():
        arrived(bias_tile, g_send.at[7])

    arrived(bias_sum, g_send.at[6])
    arrived(r4, g_send.at[5])

    arrived(bias_far, g_recv.at[6])
    near_bias, far_bias = bias_sum[0:1, :], bias_far[0:1, :]
    g_bias[:, 0:F_IN] = jnp.where(first_core, near_bias, far_bias)
    g_bias[:, F_IN:] = jnp.where(first_core, far_bias, near_bias)
    arrived(r5, g_recv.at[5])
    grads[other] = r5[...]


def spread(hidden_in, grads_h, bias_in, hidden, g_self, g_neigh, g_bias, grads_in, sems):
    moves = [
        pltpu.make_async_copy(a, b, sems.at[n])
        for n, (a, b) in enumerate(((grads_h, grads_in), (hidden_in, hidden), (bias_in, g_bias)))
    ]
    for move in moves:
        move.start()
    moves[0].wait()
    for half, target in enumerate((g_self, g_neigh)):
        for o in range(OWNERS):
            target[16 * (o // 2):16 * (o // 2) + 16, TILE * (o % 2):TILE * (o % 2) + TILE] = grads_in[
                half, o
            ].astype(F32)
    moves[1].wait()
    moves[2].wait()


def body(
    features, self_weight, neigh_weight, bias, degree, cotangent, owners, tile_rows, tile_cols, tile_count, masks
):
    vmem = pl.BlockSpec(memory_space=pltpu.VMEM)
    dma = pltpu.SemaphoreType.DMA
    hidden, grads, g_bias = pl.pallas_call(
        kernel,
        out_shape=(
            jax.ShapeDtypeStruct((SHARE, F), BF16),
            jax.ShapeDtypeStruct((NC, OWNERS, 16, TILE), BF16),
            jax.ShapeDtypeStruct((1, F), F32),
        ),
        in_specs=[pl.BlockSpec(memory_space=pl.ANY)] * 11,
        out_specs=(vmem,) * 3,
        scratch_shapes=[
            pltpu.VMEM((ROWS, F_IN), BF16),
            pltpu.VMEM((F_IN, F), BF16),
            pltpu.VMEM((F_IN, F), BF16),
            pltpu.VMEM((1, F), F32),
            pltpu.VMEM((1, SHARE), jnp.int32),
            pltpu.VMEM((SHARE, F), BF16),
            pltpu.SMEM((1, SECTIONS), jnp.int32),
            pltpu.VMEM((1, SECTIONS), jnp.int32),
            pltpu.VMEM((1, SECTIONS), jnp.int32),
            pltpu.SMEM((1, SECTIONS), jnp.int32),
            pltpu.SMEM((1, 1, SECTIONS, SLOTS), jnp.int32),
            pltpu.SMEM((1, 1, SECTIONS, SLOTS), jnp.int32),
            pltpu.SMEM((1, 1, SECTIONS), jnp.int32),
            pltpu.SMEM((SECTIONS, SLOTS), jnp.int32),
            pltpu.SMEM((RT,), jnp.int32),
            pltpu.VMEM((SECTIONS, SLOTS, TILE, TILE), jnp.int32),
            pltpu.VMEM((SECTIONS, SLOTS, TILE, TILE), BF16),
            pltpu.VMEM((CHIPS, PIECE, F_IN), BF16),
            pltpu.VMEM((2, 2, PIECE, F_IN), BF16),
            pltpu.VMEM((2, 2, PIECE, F_IN), BF16),
            pltpu.VMEM((SECTIONS, ROWS, F_IN), BF16),
            pltpu.VMEM((2, PIECE, F_IN), BF16),
            pltpu.VMEM((RT, TILE, F_IN), BF16),
            pltpu.VMEM((1 + SECTIONS * SLOTS, TILE, F_IN), F32),
            pltpu.VMEM((NZ * NYL, SHARE, F_IN), F32),
            pltpu.VMEM((NZ, SHARE, F_IN), BF16),
            pltpu.VMEM((NZ, SHARE, F_IN), BF16),
            pltpu.VMEM((NZ, SHARE, F_IN), BF16),
            pltpu.VMEM((NZ, SHARE, F_IN), BF16),
            pltpu.VMEM((SHARE, F), F32),
            pltpu.VMEM((SHARE, F_IN + F), BF16),
            pltpu.VMEM((SHARE, F_IN + F), BF16),
            pltpu.VMEM((8, F_IN), F32),
            pltpu.VMEM((8, F_IN), F32),
            pltpu.VMEM((8, F_IN), F32),
            pltpu.VMEM((8, F_IN), F32),
            pltpu.VMEM((OWNERS, 16, TILE), BF16),
            pltpu.VMEM((NX * NY, 16, TILE), BF16),
            pltpu.VMEM((16, TILE), BF16),
            pltpu.VMEM((NZ, 16, TILE), BF16),
            pltpu.VMEM((16, TILE), BF16),
            pltpu.VMEM((OWNERS, 16, TILE), BF16),
            pltpu.VMEM((OWNERS, 16, TILE), BF16),
            pltpu.VMEM((8, TILE), F32),
            pltpu.VMEM((NX * NY, 8, TILE), F32),
            pltpu.VMEM((8, TILE), F32),
            pltpu.VMEM((NZ, 8, TILE), F32),
            dma((11,)),
            dma((SECTIONS,)),
            dma,
            dma,
            dma,
            dma((5,)),
            dma,
            dma,
            dma((3,)),
            dma((2, NYH)),
            dma,
            dma((2,)),
            dma,
            dma((4,)),
            dma,
            dma((RT,)),
            dma,
            dma,
            dma((10,)),
            dma((10,)),
        ],
        compiler_params=pltpu.CompilerParams(
            collective_id=0, has_side_effects=True, vmem_limit_bytes=60 * 1024 * 1024
        ),
    )(
        features, self_weight, neigh_weight, bias.reshape(1, F), degree.reshape(1, SHARE), cotangent,
        owners, tile_rows, tile_cols, tile_count, masks.reshape(SECTIONS, SLOTS, TILE, TILE),
    )
    hidden, g_self, g_neigh, g_bias = pl.pallas_call(
        spread,
        out_shape=(
            jax.ShapeDtypeStruct((SHARE, F), BF16),
            jax.ShapeDtypeStruct((F_IN, F), F32),
            jax.ShapeDtypeStruct((F_IN, F), F32),
            jax.ShapeDtypeStruct((1, F), F32),
        ),
        in_specs=[pl.BlockSpec(memory_space=pl.ANY)] * 3,
        out_specs=(
            pl.BlockSpec(memory_space=pl.ANY), vmem, vmem, pl.BlockSpec(memory_space=pl.ANY)
        ),
        scratch_shapes=[pltpu.VMEM((NC, OWNERS, 16, TILE), BF16), pltpu.SemaphoreType.DMA((3,))],
        compiler_params=pltpu.CompilerParams(vmem_limit_bytes=60 * 1024 * 1024),
    )(hidden, grads, g_bias)
    return hidden, g_self, g_neigh, g_bias.reshape(F)


def solution(mesh):
    return jax.shard_map(
        body,
        mesh=mesh,
        in_specs=(
            P("rows", None),
            P(),
            P(),
            P(),
            P(("rows", "rep")),
            P(("rows", "rep"), None),
            P("rep", None),
            P("rows", "rep", None, None),
            P("rows", "rep", None, None),
            P("rows", "rep", None),
            P("rows", "rep", None, None, None, None),
        ),
        out_specs=(P(("rows", "rep"), None), P(), P(), P()),
        check_vma=False,
    )
```

time: 82.9 us -> 75.9 us (0.916)
  local copies, waits for them, and re-layouts: 4.25 us -> 0 us
  Pallas kernels: 77.8 us -> 75.1 us
    pallas_call x1, Pallas kernels: 77.8 us -> 72.7 us  [body(): pl.pallas_call(kernel, out_shape=(jax.ShapeDtypeStruct((SHARE, F), BF16),...]
    unnamed x2 -> x0, local copies, waits for them, and re-layouts: 2.56 us -> none
    pallas_call x0 -> x1, Pallas kernels: none -> 2.35 us  [body(): pl.pallas_call(spread, out_shape=(jax.ShapeDtypeStruct((SHARE, F), BF16),...]
    squeeze x1 -> x0, local copies, waits for them, and re-layouts: 1.69 us -> none  [body(): return (hidden, grads[0], grads[1], g_bias.reshape(F))]
where the time goes in v3:
time: 75.9 us; the launch traced here: 75.7 us
  Pallas kernels  75.1 us (99%)
    pallas_call x1, Pallas kernels, body(): pl.pallas_call(kernel, out_shape=(jax.ShapeDtypeStruct((SHARE, F), BF16),...  72.7 us
    pallas_call x1, Pallas kernels, body(): pl.pallas_call(spread, out_shape=(jax.ShapeDtypeStruct((SHARE, F), BF16),...  2.35 us

profile of v3, /device:TPU:1, one launch (start us, length us, event | category | flops | bytes accessed | tf_op | source)
XLA Modules:
  0.0 75.7 jit_solution(12239277799168730619)
XLA Ops:
  0.6 72.7 %shard_map.138 = (bf16[32,256]{1,0:T(8,128)(2,1)}, bf16[2,16,16,128]{3,2,1,0:T(8,128)(2,1)}, f32[1,256]{1,0:T(1,128)}) custom-call(bf16[768,128]{1,0:T(8,128)(2,1)} %feat_h.1, bf16[128,256]{1,0:T(8,128)(2,1)} %w_self_h.1, bf16[128,256]{1,0:T(8,128)(2,1)} %w_neigh_h.1, f32[1,256]{1,0:T(1,128)} %bitcast.5, s32[1,32]{1,0:T(1,128)} %bitcast.6, ...), custom_call_target="tpu_custom_call" | custom-call | tf_op jit(solution)/shard_map/pallas_call | solution.py:445
  73.4 2.4 %shard_map.139 = (bf16[32,256]{1,0:T(8,128)(2,1)}, f32[128,256]{1,0:T(8,128)}, f32[128,256]{1,0:T(8,128)}, f32[1,256]{1,0:T(1,128)}) custom-call(bf16[32,256]{1,0:T(8,128)(2,1)} %get-tuple-element.11.hidden_in, bf16[2,16,16,128]{3,2,1,0:T(8,128)(2,1)} %get-tuple-element.12.grads_h, f32[1,256]{1,0:T(1,128)} %get-tuple-element.13.bias_in), custom_call_target="tpu_custom_call" | custom-call | tf_op jit(solution)/shard_map/pallas_call | solution.py:530

commit v4 on v3

--- a/solution.py
+++ b/solution.py
@@ -33,7 +33,7 @@
     before, last, mask_raw, mask_low, got1, give_core, got_core, feats, part_mate, tiles, sums, acc, y_out, y_in,
     z_out, z_in, pre_own, pair_out, pair_in, bias_out, bias_in, bias_sum, bias_far,
     m1, r1, m3, r3, m4, r4, r5, bias_tile, rb, m3b, r3b,
-    in_sem, mask_sem, o_send, o_recv, o_copy, s_send, s1_recv, core_recv, yrecv, xrecv, far_recv, relay_recv, half_send, half_recv,
+    in_sem, mask_sem, o_send, o_recv, o_copy, s_send, s1_recv, core_recv, yrecv, xrecv, half_send, half_recv,
     yl_send, yl_recv, z_send, z_recv, g_send, g_recv,
 ):
     row, rep = lax.axis_index("rows"), lax.axis_index("rep")
@@ -72,8 +72,7 @@
         (tcnt_h, tcnt), (w_neigh_h, w_neigh), (degree_h, degree), (cot_h, cot),
     )
     loads = [pltpu.make_async_copy(a, b, in_sem.at[n]) for n, (a, b) in enumerate(pairs)]
-    for copy in loads:
-        copy.start()
+    loads[0].start()
     barrier = pltpu.get_barrier_semaphore()
 
     def greet(device):
@@ -85,6 +84,8 @@
         greet(at_plane(x_, y_))
     greet(core_mate)
 
+    for copy in loads[1:]:
+        copy.start()
     mask_copies = [
         pltpu.make_async_copy(masks.at[s], mask_raw.at[s], mask_sem.at[s]) for s in range(SECTIONS)
     ]
@@ -177,10 +178,6 @@
         start = pl.multiple_of((x_ * NYH + yh_) * PIECE, 16)
         return feats.at[pl.ds(2 * core, 2), pl.ds(start, PIECE), :]
 
-    def half(t, x_, yh_):
-        start = pl.multiple_of((x_ * NYH + yh_) * PIECE, 16)
-        return feats.at[2 * core + t, pl.ds(start, PIECE), :]
-
     right, left, far = lax.rem(x + 1, NX), lax.rem(x + 3, NX), lax.rem(x + 2, NX)
     to_right, to_left, to_far = (dev(x_, yh, core, z, yl) for x_ in (right, left, far))
     beside = lax.rem(yh + 1 - 2 * yl + NYH, NYH)
@@ -189,35 +186,20 @@
     send(here, here, s_send.at[2], yrecv.at[1], dev(x, near, core, z, yl))
 
     def sideways(n, yh_):
-        send(part(x, yh_), part(x, yh_), s_send.at[3], xrecv.at[0, n], to_right)
-        send(part(x, yh_), part(x, yh_), s_send.at[3], xrecv.at[1, n], to_left)
-
-    def relay(n, yh_):
-        arrived(part(left, yh_), xrecv.at[0, n])
-        send(half(0, left, yh_), half(0, left, yh_), s_send.at[4], relay_recv.at[0], to_right)
-        arrived(part(right, yh_), xrecv.at[1, n])
-        send(half(1, right, yh_), half(1, right, yh_), s_send.at[4], relay_recv.at[1], to_left)
+        for k, device in enumerate((to_far, to_right, to_left)):
+            send(part(x, yh_), part(x, yh_), s_send.at[3], xrecv.at[k], device)
 
     sideways(0, yh)
     arrived(part(x, near), yrecv.at[0])
     sideways(1, near)
-    relay(0, yh)
     arrived(part(x, beside), yrecv.at[1])
     sideways(2, beside)
     arrived(part(x, across), yrecv.at[2])
-    send(part(x, across), part(x, across), s_send.at[3], far_recv, to_far)
     sideways(3, across)
     send(line(x), line(x), half_send, half_recv.at[0], core_mate)
-    relay(1, near)
-    relay(2, beside)
-    arrived(part(left, across), xrecv.at[0, 3])
-    send(line(left), line(left), half_send, half_recv.at[1], core_mate)
-    arrived(part(right, across), xrecv.at[1, 3])
-    send(line(right), line(right), half_send, half_recv.at[2], core_mate)
-    arrived(part(far, across), far_recv)
-    arrived(feats.at[0, pl.ds(0, 3 * PIECE), :], relay_recv.at[0])
-    arrived(feats.at[0, pl.ds(0, 3 * PIECE), :], relay_recv.at[1])
-    send(line(far), line(far), half_send, half_recv.at[3], core_mate)
+    for n, source in ((1, left), (2, right), (0, far)):
+        arrived(line(source), xrecv.at[n])
+        send(line(source), line(source), half_send, half_recv.at[n or 3], core_mate)
 
     def multiply(t):
         s = lax.rem(2 * core + t, SECTIONS)
@@ -239,32 +221,27 @@
     multiply(2)
     multiply(3)
 
-    def second_half(step, carry):
-        r = lax.rem(lax.div(z, 2) + 1 + step, RT)
+    order = [lax.rem(lax.div(z, 2) + step, RT) for step in (3, 2, 4, 1, 5, 0)]
+    for r in order:
         acc[pl.ds(4 * r, 4)] = sums[last[r]].reshape(4, SHARE, F_IN)
         for h in range(2):
             y_out[2 * r + h] = acc[4 * r + 2 * h + 1 - yl].astype(BF16)
         send(y_out.at[pl.ds(2 * r, 2)], y_in.at[pl.ds(2 * r, 2)], yl_send, yl_recv.at[r], yl_mate)
-        return carry
-
-    lax.fori_loop(0, RT, second_half, 0)
-
-    def to_z(step, carry):
-        r = lax.rem(lax.div(z, 2) + 1 + step, RT)
+
+    for step, r in enumerate(order):
         arrived(y_in.at[pl.ds(2 * r, 2)], yl_recv.at[r])
         for h in range(2):
             z_ = 2 * r + h
             both = acc[4 * r + 2 * h + yl] + y_in[z_].astype(F32)
             acc[4 * r + 2 * h + yl] = both
             z_out[z_] = both.astype(BF16)
-
-            @pl.when(z_ != z)
-            def _():
+            if step < RT - 1:
                 send(z_out.at[z_], z_in.at[z], z_send, z_recv, dev(x, yh, core, z_, yl))
-
-        return carry
-
-    lax.fori_loop(0, RT, to_z, 0)
+            else:
+                @pl.when(z_ != z)
+                def _(z_=z_):
+                    send(z_out.at[z_], z_in.at[z], z_send, z_recv, dev(x, yh, core, z_, yl))
+
     z_in[z] = jnp.zeros((SHARE, F_IN), BF16)
     lanes = lax.broadcasted_iota(jnp.int32, (SHARE, SHARE), 1)
     subs = lax.broadcasted_iota(jnp.int32, (SHARE, SHARE), 0)
@@ -383,8 +360,7 @@
     arrived(got1.at[pl.ds(0, CHIPS - 1)], s_send.at[0])
     arrived(give_core, s_send.at[1])
     arrived(feats.at[0, pl.ds(0, 6 * PIECE), :], s_send.at[2])
-    arrived(feats.at[pl.ds(0, 3), pl.ds(0, 6 * PIECE), :], s_send.at[3])
-    arrived(feats.at[0, pl.ds(0, 6 * PIECE), :], s_send.at[4])
+    arrived(feats.at[pl.ds(0, 3), pl.ds(0, 8 * PIECE), :], s_send.at[3])
     arrived(feats.at[pl.ds(0, 2)], half_send)
     arrived(y_out, yl_send)
     arrived(z_out.at[pl.ds(0, NZ - 1)], z_send)
@@ -504,13 +480,11 @@
             dma,
             dma,
             dma,
-            dma((5,)),
+            dma((4,)),
             dma,
             dma,
             dma((3,)),
-            dma((2, NYH)),
-            dma,
-            dma((2,)),
+            dma((3,)),
             dma,
             dma((4,)),
             dma,

time: 75.9 us -> 73.4 us (0.967)
  Pallas kernels: 75.1 us -> 72.6 us
    pallas_call x1, Pallas kernels: 72.7 us -> 70.2 us  [body(): pl.pallas_call(kernel, out_shape=(jax.ShapeDtypeStruct((SHARE, F), BF16),...]
where the time goes in v4:
time: 73.4 us; the launch traced here: 73.2 us
  Pallas kernels  72.6 us (99%)
    pallas_call x1, Pallas kernels, body(): pl.pallas_call(kernel, out_shape=(jax.ShapeDtypeStruct((SHARE, F), BF16),...  70.2 us
    pallas_call x1, Pallas kernels, body(): pl.pallas_call(spread, out_shape=(jax.ShapeDtypeStruct((SHARE, F), BF16),...  2.35 us

profile of v4, /device:TPU:1, one launch (start us, length us, event | category | flops | bytes accessed | tf_op | source)
XLA Modules:
  0.0 73.2 jit_solution(15938877742224336214)
XLA Ops:
  0.6 70.2 %shard_map.138 = (bf16[32,256]{1,0:T(8,128)(2,1)}, bf16[2,16,16,128]{3,2,1,0:T(8,128)(2,1)}, f32[1,256]{1,0:T(1,128)}) custom-call(bf16[768,128]{1,0:T(8,128)(2,1)} %feat_h.1, bf16[128,256]{1,0:T(8,128)(2,1)} %w_self_h.1, bf16[128,256]{1,0:T(8,128)(2,1)} %w_neigh_h.1, f32[1,256]{1,0:T(1,128)} %bitcast.5, s32[1,32]{1,0:T(1,128)} %bitcast.6, ...), custom_call_target="tpu_custom_call" | custom-call | tf_op jit(solution)/shard_map/pallas_call | solution.py:421
  70.9 2.4 %shard_map.139 = (bf16[32,256]{1,0:T(8,128)(2,1)}, f32[128,256]{1,0:T(8,128)}, f32[128,256]{1,0:T(8,128)}, f32[1,256]{1,0:T(1,128)}) custom-call(bf16[32,256]{1,0:T(8,128)(2,1)} %get-tuple-element.11.hidden_in, bf16[2,16,16,128]{3,2,1,0:T(8,128)(2,1)} %get-tuple-element.12.grads_h, f32[1,256]{1,0:T(1,128)} %get-tuple-element.13.bias_in), custom_call_target="tpu_custom_call" | custom-call | tf_op jit(solution)/shard_map/pallas_call | solution.py:504

commit v5 on v4

--- a/solution.py
+++ b/solution.py
@@ -30,7 +30,7 @@
     feat_h, w_self_h, w_neigh_h, bias_h, degree_h, cot_h, owners_h, trow_h, tcol_h, tcnt_h, masks,
     hidden, grads, g_bias,
     feat, w_self, w_neigh, bias, degree, cot, owners, owners_v, owners_mate_v, owners_mate, trow, tcol, tcnt,
-    before, last, mask_raw, mask_low, got1, give_core, got_core, feats, part_mate, tiles, sums, acc, y_out, y_in,
+    before, last, mask_raw, mask_low, got1, give_core, got_core, feats, part_mate, tiles, prods, sums, acc, y_out, y_in,
     z_out, z_in, pre_own, pair_out, pair_in, bias_out, bias_in, bias_sum, bias_far,
     m1, r1, m3, r3, m4, r4, r5, bias_tile, rb, m3b, r3b,
     in_sem, mask_sem, o_send, o_recv, o_copy, s_send, s1_recv, core_recv, yrecv, xrecv, half_send, half_recv,
@@ -207,11 +207,15 @@
             tiles[c] = feats[s, TILE * c:TILE * c + TILE, :]
 
         def one(k, carry):
-            product = jnp.dot(mask_low[s, k], tiles[tcol[0, 0, s, k]], preferred_element_type=F32)
-            sums[1 + t * SLOTS + k] = product + sums[before[t, k]]
+            prods[k] = jnp.dot(mask_low[s, k], tiles[tcol[0, 0, s, k]], preferred_element_type=F32)
             return carry
 
+        def link(k, carry):
+            sums[1 + t * SLOTS + k] = prods[k] + sums[before[t, k]]
+            return carry
+
         lax.fori_loop(0, SLOTS, one, 0, unroll=8)
+        lax.fori_loop(0, SLOTS, link, 0)
 
     multiply(0)
     multiply(1)
@@ -451,6 +455,7 @@
             pltpu.VMEM((SECTIONS, ROWS, F_IN), BF16),
             pltpu.VMEM((2, PIECE, F_IN), BF16),
             pltpu.VMEM((RT, TILE, F_IN), BF16),
+            pltpu.VMEM((SLOTS, TILE, F_IN), F32),
             pltpu.VMEM((1 + SECTIONS * SLOTS, TILE, F_IN), F32),
             pltpu.VMEM((NZ * NYL, SHARE, F_IN), F32),
             pltpu.VMEM((NZ, SHARE, F_IN), BF16),

time: 73.4 us -> 74 us (level)
  no operation moved by 1% of the time
where the time goes in v5:
time: 74 us; the launch traced here: 73.8 us
  Pallas kernels  73.1 us (99%)
    pallas_call x1, Pallas kernels, body(): pl.pallas_call(kernel, out_shape=(jax.ShapeDtypeStruct((SHARE, F), BF16),...  70.8 us
    pallas_call x1, Pallas kernels, body(): pl.pallas_call(spread, out_shape=(jax.ShapeDtypeStruct((SHARE, F), BF16),...  2.35 us

profile of v5, /device:TPU:1, one launch (start us, length us, event | category | flops | bytes accessed | tf_op | source)
XLA Modules:
  0.0 73.8 jit_solution(15295449295390502896)
XLA Ops:
  0.6 70.8 %shard_map.138 = (bf16[32,256]{1,0:T(8,128)(2,1)}, bf16[2,16,16,128]{3,2,1,0:T(8,128)(2,1)}, f32[1,256]{1,0:T(1,128)}) custom-call(bf16[768,128]{1,0:T(8,128)(2,1)} %feat_h.1, bf16[128,256]{1,0:T(8,128)(2,1)} %w_self_h.1, bf16[128,256]{1,0:T(8,128)(2,1)} %w_neigh_h.1, f32[1,256]{1,0:T(1,128)} %bitcast.5, s32[1,32]{1,0:T(1,128)} %bitcast.6, ...), custom_call_target="tpu_custom_call" | custom-call | tf_op jit(solution)/shard_map/pallas_call | solution.py:425
  71.4 2.4 %shard_map.139 = (bf16[32,256]{1,0:T(8,128)(2,1)}, f32[128,256]{1,0:T(8,128)}, f32[128,256]{1,0:T(8,128)}, f32[1,256]{1,0:T(1,128)}) custom-call(bf16[32,256]{1,0:T(8,128)(2,1)} %get-tuple-element.11.hidden_in, bf16[2,16,16,128]{3,2,1,0:T(8,128)(2,1)} %get-tuple-element.12.grads_h, f32[1,256]{1,0:T(1,128)} %get-tuple-element.13.bias_in), custom_call_target="tpu_custom_call" | custom-call | tf_op jit(solution)/shard_map/pallas_call | solution.py:509

commit v6 on v5

--- a/solution.py
+++ b/solution.py
@@ -91,13 +91,8 @@
     ]
     for copy in mask_copies:
         copy.start()
-    loads[0].wait()
-    loads[1].wait()
-    loads[2].wait()
-    got1[chip] = feat[pl.ds(pl.multiple_of(chip * PIECE, 16), PIECE), :]
     pl.semaphore_wait(barrier, len(plane) + NZ)
 
-    send(owners_v, owners_mate_v, o_send, o_recv, yl_mate)
     near, across = lax.rem(yh + 2 * yl + NYH - 1, NYH), lax.rem(yh + 2, NYH)
     shares = [(2, across, 1 - yl), (1, across, 1 - yl), (3, across, 1 - yl), (0, across, 1 - yl)]
     shares += [(dx, near, yl_) for dx in (2, 1, 3, 0) for yl_ in range(NYL)]
@@ -106,11 +101,15 @@
         x_ = lax.rem(x + dx, NX)
         there = x_ * NYH + yh_
         send(
-            feat.at[pl.ds(pl.multiple_of(there * PIECE, 16), PIECE), :],
+            feat_h.at[pl.ds(pl.multiple_of(there * PIECE, 16), PIECE), :],
             got1.at[chip], s_send.at[0], s1_recv, dev(x_, yh_, core, z, yl_),
         )
 
-    for copy in loads[3:]:
+    loads[1].wait()
+    send(owners_v, owners_mate_v, o_send, o_recv, yl_mate)
+    loads[0].wait()
+    got1[chip] = feat[pl.ds(pl.multiple_of(chip * PIECE, 16), PIECE), :]
+    for copy in loads[2:]:
         copy.wait()
     own = feat[pl.ds(pl.multiple_of(rep * SHARE, 16), SHARE), :]
     pre_own[...] = jnp.dot(own, w_self[...], preferred_element_type=F32) + bias[...]

time: 74 us -> 74.2 us (level)
  no operation moved by 1% of the time
where the time goes in v6:
time: 74.2 us; the launch traced here: 74 us
  Pallas kernels  73.4 us (99%)
    pallas_call x1, Pallas kernels, body(): pl.pallas_call(kernel, out_shape=(jax.ShapeDtypeStruct((SHARE, F), BF16),...  71 us
    pallas_call x1, Pallas kernels, body(): pl.pallas_call(spread, out_shape=(jax.ShapeDtypeStruct((SHARE, F), BF16),...  2.35 us

profile of v6, /device:TPU:1, one launch (start us, length us, event | category | flops | bytes accessed | tf_op | source)
XLA Modules:
  0.0 74.0 jit_solution(9252049005504922184)
XLA Ops:
  0.6 71.0 %shard_map.138 = (bf16[32,256]{1,0:T(8,128)(2,1)}, bf16[2,16,16,128]{3,2,1,0:T(8,128)(2,1)}, f32[1,256]{1,0:T(1,128)}) custom-call(bf16[768,128]{1,0:T(8,128)(2,1)} %feat_h.1, bf16[128,256]{1,0:T(8,128)(2,1)} %w_self_h.1, bf16[128,256]{1,0:T(8,128)(2,1)} %w_neigh_h.1, f32[1,256]{1,0:T(1,128)} %bitcast.5, s32[1,32]{1,0:T(1,128)} %bitcast.6, ...), custom_call_target="tpu_custom_call" | custom-call | tf_op jit(solution)/shard_map/pallas_call | solution.py:424
  71.6 2.4 %shard_map.139 = (bf16[32,256]{1,0:T(8,128)(2,1)}, f32[128,256]{1,0:T(8,128)}, f32[128,256]{1,0:T(8,128)}, f32[1,256]{1,0:T(1,128)}) custom-call(bf16[32,256]{1,0:T(8,128)(2,1)} %get-tuple-element.11.hidden_in, bf16[2,16,16,128]{3,2,1,0:T(8,128)(2,1)} %get-tuple-element.12.grads_h, f32[1,256]{1,0:T(1,128)} %get-tuple-element.13.bias_in), custom_call_target="tpu_custom_call" | custom-call | tf_op jit(solution)/shard_map/pallas_call | solution.py:508
